TPU v7x, 128 devices: a whole 4x4x4 slice. The times are simulated.
128 devices in a mesh: ctx: 8 (over z_hi, x), fsdp: 16 (over y, z_lo, core).
Axes of the slice: x: 4, y: 4, z: 4 (z_hi: 2, z_lo: 2; z = z_hi * 2 + z_lo), core: 2. Of those that a mesh axis runs over, the one named last changes fastest.
Arguments:
- inputs: bfloat16 [16, 1024, 1536], P('fsdp', 'ctx'), may hold values from -6 to 6
- block_order: int32 [16], replicated, may hold values from 0 to 15, each once
- routes: int32 [16, 1024, 8], P('fsdp', 'ctx'), may hold values from 0 to 39, all different within a row; in each aligned block of 128 rows (0 to 127, 128 to 255, ..., all dimensions but the last counted through in order) at most 32 rows name the same one
- pre_gain: bfloat16 [1536], P('fsdp'), may hold values from 0.5 to 1.5
- w_query: bfloat16 [1536, 1536], P('fsdp'), may hold values from -0.4375 to 0.4375
- w_key: bfloat16 [1536, 512], P('fsdp'), may hold values from -0.4375 to 0.4375
- w_value: bfloat16 [1536, 512], P('fsdp'), may hold values from -0.15625 to 0.15625
- w_out: bfloat16 [1536, 1536], P('fsdp'), may hold values from -6 to 6
- w_router: bfloat16 [1536, 40], P('fsdp'), may hold values from -0.079589844 to 0.079589844
- mid_gain: bfloat16 [1536], P('fsdp'), may hold values from 0.5 to 1.5
- w_gate: bfloat16 [40, 1536, 512], P('ctx', 'fsdp'), may hold values from -0.15625 to 0.15625
- w_up: bfloat16 [40, 1536, 512], P('ctx', 'fsdp'), may hold values from -0.15625 to 0.15625
- w_down: bfloat16 [40, 512, 1536], P('ctx', 'fsdp'), may hold values from -6 to 6
- cotangent: bfloat16 [16, 1024, 1536], P('fsdp', 'ctx'), may hold values from -6 to 6
Outputs:
- output: bfloat16 [16, 1024, 1536], P('fsdp', 'ctx')
- grad_input: bfloat16 [16, 1024, 1536], P('fsdp', 'ctx')
- grad_pre: float32 [1536], P('fsdp')
- grad_query: float32 [1536, 1536], P('fsdp')
- grad_key: float32 [1536, 512], P('fsdp')
- grad_value: float32 [1536, 512], P('fsdp')
- grad_out: float32 [1536, 1536], P('fsdp')
- grad_router: float32 [1536, 40], P('fsdp')
- grad_mid: float32 [1536], P('fsdp')
- grad_gate: float32 [40, 1536, 512], P('ctx', 'fsdp')
- grad_up: float32 [40, 1536, 512], P('ctx', 'fsdp')
- grad_down: float32 [40, 512, 1536], P('ctx', 'fsdp')
Inputs may be any that keep to these rules, and one draw needn't show every extreme that they name: `block_order`: each of 0 to 15 appears once. `routes`: each token names 8 different experts. Among the 128 tokens of one sequence on one device, no expert is named by more than 32 tokens, a bound that some block reaches.
All inputs are finite; a program needn't handle non-finite values.
Results may differ from a plain program's by a relative error of at most 0.028.
Values may be sent and summed in bfloat16 or wider, within the bound.
No kernel may reach another device: no remote copies, remote signals or barrier semaphores. Data moves between devices by JAX's collectives and lax.ppermute only.
A program may use at most 192 MiB of HBM per device.

v0:
```python
import jax
import jax.numpy as jnp
from jax import lax
from jax.sharding import PartitionSpec as P

HEADS = 24
KV_HEADS = 8
HEAD_DIM = 64
EXPERTS = 40
TOP = 8
SEQ_LEN = 1024


EPSILON = 1e-06
SCORE_SCALE = 0.015625
RESIDUAL_SCALE = 0.22
THETA_BASE = 10000.0
PRECISE = lax.Precision.HIGHEST


def rotary_tables(positions):
    half_dim = HEAD_DIM // 2
    freqs = THETA_BASE ** (-2.0 * jnp.arange(half_dim, dtype=jnp.float32) / HEAD_DIM)
    angles = positions.astype(jnp.float32)[:, None] * freqs[None, :]
    cosine_table = jnp.cos(angles)
    sine_table = jnp.sin(angles)
    return (
        jnp.concatenate([cosine_table, cosine_table], -1),
        jnp.concatenate([sine_table, sine_table], -1),
    )


def rotate(values, cosine_table, sine_table, turn_sign):
    half_dim = values.shape[-1] // 2
    turned = jnp.concatenate([-values[..., half_dim:], values[..., :half_dim]], -1)
    return values * cosine_table[:, None, :] + turn_sign * turned * sine_table[:, None, :]


def norm_forward(values, gain_vec):
    scaler = lax.rsqrt(jnp.mean(values * values, axis=-1, keepdims=True) + EPSILON)
    normed = values * scaler
    return (normed * gain_vec, normed, scaler)


def norm_backward(grad_out, gain_vec, normed, scaler):
    grad_gain = jnp.sum(grad_out * normed, axis=0)
    inner = grad_out * gain_vec
    grad_in = scaler * (inner - normed * jnp.mean(inner * normed, axis=-1, keepdims=True))
    return (grad_in, grad_gain)


def on_device(
    inputs,
    block_order,
    routes,
    pre_gain,
    w_query,
    w_key,
    w_value,
    w_out,
    w_router,
    mid_gain,
    w_gate,
    w_up,
    w_down,
    cotangent,
):
    seq_count, tok_count, feature_dim = inputs.shape
    row_count = seq_count * tok_count
    ctx_count = lax.axis_size("ctx")
    ctx_index = lax.axis_index("ctx")
    head_groups = HEADS // KV_HEADS
    kv_width = KV_HEADS * HEAD_DIM
    gathered = (
        lax.all_gather(pre_gain, "fsdp", axis=0, tiled=True),
        lax.all_gather(w_query, "fsdp", axis=0, tiled=True),
        lax.all_gather(w_key, "fsdp", axis=0, tiled=True),
        lax.all_gather(w_value, "fsdp", axis=0, tiled=True),
        lax.all_gather(w_out, "fsdp", axis=0, tiled=True),
        lax.all_gather(w_router, "fsdp", axis=0, tiled=True),
        lax.all_gather(mid_gain, "fsdp", axis=0, tiled=True),
    )
    pre_full, query_full, key_full, value_full, out_full, router_full, mid_full = gathered
    pre_vec = pre_full.astype(jnp.float32)
    mid_vec = mid_full.astype(jnp.float32)
    router_mat = router_full.astype(jnp.float32)
    block_span = SEQ_LEN // block_order.shape[0]
    offsets = jnp.arange(SEQ_LEN, dtype=jnp.int32)
    key_positions = (
        jnp.repeat(block_order, block_span, total_repeat_length=SEQ_LEN) * block_span
        + offsets % block_span
    )
    query_positions = lax.dynamic_slice_in_dim(key_positions, ctx_index * tok_count, tok_count)
    visible = key_positions[None, :] <= query_positions[:, None]
    cosine_table, sine_table = rotary_tables(query_positions)
    inputs_wide = inputs.reshape(row_count, feature_dim).astype(jnp.float32)
    normed1, unit1, scaler1 = norm_forward(inputs_wide, pre_vec)
    normed1_low = normed1.astype(jnp.bfloat16)
    query_raw = jnp.dot(normed1_low, query_full, preferred_element_type=jnp.float32)
    key_raw = jnp.dot(normed1_low, key_full, preferred_element_type=jnp.float32)
    value_raw = jnp.dot(normed1_low, value_full, preferred_element_type=jnp.float32)
    query_low = rotate(
        query_raw.reshape(seq_count, tok_count, HEADS, HEAD_DIM), cosine_table, sine_table, 1.0
    ).astype(jnp.bfloat16)
    query_split = query_low.reshape(seq_count, tok_count, KV_HEADS, head_groups, HEAD_DIM)
    key_low = rotate(
        key_raw.reshape(seq_count, tok_count, KV_HEADS, HEAD_DIM), cosine_table, sine_table, 1.0
    ).astype(jnp.bfloat16)
    key_low = key_low.reshape(seq_count, tok_count, kv_width)
    value_low = value_raw.astype(jnp.bfloat16).reshape(seq_count, tok_count, kv_width)
    keys_all, values_all = (
        lax.all_gather(key_low, "ctx", axis=1, tiled=True),
        lax.all_gather(value_low, "ctx", axis=1, tiled=True),
    )

    def masked_scores(keys_whole):
        keys_split = keys_whole.reshape(seq_count, SEQ_LEN, KV_HEADS, HEAD_DIM)
        raw_scores = (
            jnp.einsum(
                "sqjgd,skjd->sjgqk", query_split, keys_split, preferred_element_type=jnp.float32
            )
            * SCORE_SCALE
        )
        return jnp.where(visible, raw_scores, -1e30)

    scores = masked_scores(keys_all)
    top_score = jnp.max(scores, axis=-1, keepdims=True)
    expo = jnp.exp(scores - top_score)
    total = jnp.sum(expo, axis=-1, keepdims=True)
    log_total = top_score + jnp.log(total)
    probs_low = (expo / total).astype(jnp.bfloat16)
    values_split = values_all.reshape(seq_count, SEQ_LEN, KV_HEADS, HEAD_DIM)
    attended = jnp.einsum(
        "sjgqk,skjd->sqjgd", probs_low, values_split, preferred_element_type=jnp.float32
    )
    attended_low = attended.reshape(row_count, HEADS * HEAD_DIM).astype(jnp.bfloat16)
    mixed = inputs_wide + RESIDUAL_SCALE * jnp.dot(
        attended_low, out_full, preferred_element_type=jnp.float32
    )
    normed2, unit2, scaler2 = norm_forward(mixed, mid_vec)
    normed2_low = normed2.astype(jnp.bfloat16)
    normed2_wide = normed2_low.astype(jnp.float32)
    logits = jnp.dot(normed2_wide, router_mat, precision=PRECISE)
    route_rows = routes.reshape(row_count, TOP)
    choose = (route_rows[:, :, None] == jnp.arange(EXPERTS, dtype=jnp.int32)[None, None, :]).astype(
        jnp.float32
    )
    picked = jnp.einsum("tke,te->tk", choose, logits, precision=PRECISE)
    gates = jax.nn.softmax(picked, axis=-1)
    exp_here = EXPERTS // ctx_count
    capacity = seq_count * (tok_count * TOP * 5 // (4 * EXPERTS))
    total_slots = exp_here * ctx_count * capacity
    expert_ids = route_rows.reshape(row_count * TOP)
    onehot = (expert_ids[:, None] == jnp.arange(EXPERTS, dtype=jnp.int32)[None, :]).astype(
        jnp.int32
    )
    ranks = jnp.sum(jnp.cumsum(onehot, axis=0) * onehot, axis=1) - 1
    slot_ids = (expert_ids % exp_here * ctx_count + expert_ids // exp_here) * capacity + ranks
    source = (
        jnp.zeros((total_slots,), jnp.int32)
        .at[slot_ids]
        .set(jnp.arange(row_count * TOP, dtype=jnp.int32))
    )
    filled = jnp.zeros((total_slots,), jnp.bfloat16).at[slot_ids].set(1.0)
    send_rows = (normed2_low[source // TOP] * filled[:, None]).reshape(
        exp_here, ctx_count, capacity, feature_dim
    )
    received = lax.all_to_all(send_rows, "ctx", split_axis=1, concat_axis=1, tiled=True).reshape(
        exp_here, ctx_count * capacity, feature_dim
    )
    gate_full, up_full, down_full = (
        lax.all_gather(w_gate, "fsdp", axis=1, tiled=True),
        lax.all_gather(w_up, "fsdp", axis=1, tiled=True),
        lax.all_gather(w_down, "fsdp", axis=1, tiled=True),
    )
    gate_pre = jnp.einsum("end,edf->enf", received, gate_full, preferred_element_type=jnp.float32)
    up_pre = jnp.einsum("end,edf->enf", received, up_full, preferred_element_type=jnp.float32)
    sigm = jax.nn.sigmoid(gate_pre)
    activated = gate_pre * sigm
    hidden_low = (activated * up_pre).astype(jnp.bfloat16)
    result_low = jnp.einsum(
        "enf,efd->end", hidden_low, down_full, preferred_element_type=jnp.float32
    ).astype(jnp.bfloat16)
    returned = lax.all_to_all(
        result_low.reshape(exp_here, ctx_count, capacity, feature_dim),
        "ctx",
        split_axis=1,
        concat_axis=1,
        tiled=True,
    )
    expert_rows = (
        returned.reshape(total_slots, feature_dim)[slot_ids]
        .astype(jnp.float32)
        .reshape(row_count, TOP, feature_dim)
    )
    final = mixed + RESIDUAL_SCALE * jnp.sum(gates[:, :, None] * expert_rows, axis=1)
    output = final.astype(jnp.bfloat16).reshape(seq_count, tok_count, feature_dim)
    grad_final = cotangent.reshape(row_count, feature_dim).astype(jnp.float32)
    grad_rows = (
        (RESIDUAL_SCALE * gates[:, :, None] * grad_final[:, None, :])
        .astype(jnp.bfloat16)
        .reshape(row_count * TOP, feature_dim)
    )
    grad_gates = RESIDUAL_SCALE * jnp.sum(expert_rows * grad_final[:, None, :], axis=-1)
    grad_send = (grad_rows[source] * filled[:, None]).reshape(
        exp_here, ctx_count, capacity, feature_dim
    )
    grad_recv = lax.all_to_all(grad_send, "ctx", split_axis=1, concat_axis=1, tiled=True).reshape(
        exp_here, ctx_count * capacity, feature_dim
    )
    grad_hidden = jnp.einsum(
        "end,efd->enf", grad_recv, down_full, preferred_element_type=jnp.float32
    )
    grad_down_full = jnp.einsum(
        "enf,end->efd", hidden_low, grad_recv, preferred_element_type=jnp.float32
    )
    grad_gate_pre = (grad_hidden * up_pre * sigm * (1.0 + gate_pre * (1.0 - sigm))).astype(
        jnp.bfloat16
    )
    grad_up_pre = (grad_hidden * activated).astype(jnp.bfloat16)
    grad_gate_full = jnp.einsum(
        "end,enf->edf", received, grad_gate_pre, preferred_element_type=jnp.float32
    )
    grad_up_full = jnp.einsum(
        "end,enf->edf", received, grad_up_pre, preferred_element_type=jnp.float32
    )
    grad_slots = jnp.einsum(
        "enf,edf->end", grad_gate_pre, gate_full, preferred_element_type=jnp.float32
    )
    grad_slots = (
        grad_slots
        + jnp.einsum("enf,edf->end", grad_up_pre, up_full, preferred_element_type=jnp.float32)
    ).astype(jnp.bfloat16)
    grad_back = lax.all_to_all(
        grad_slots.reshape(exp_here, ctx_count, capacity, feature_dim),
        "ctx",
        split_axis=1,
        concat_axis=1,
        tiled=True,
    )
    grad_normed2 = jnp.sum(
        grad_back.reshape(total_slots, feature_dim)[slot_ids]
        .astype(jnp.float32)
        .reshape(row_count, TOP, feature_dim),
        axis=1,
    )
    expert_grads = (
        lax.psum_scatter(
            grad_gate_full.astype(jnp.bfloat16), "fsdp", scatter_dimension=1, tiled=True
        ).astype(jnp.float32),
        lax.psum_scatter(
            grad_up_full.astype(jnp.bfloat16), "fsdp", scatter_dimension=1, tiled=True
        ).astype(jnp.float32),
        lax.psum_scatter(
            grad_down_full.astype(jnp.bfloat16), "fsdp", scatter_dimension=1, tiled=True
        ).astype(jnp.float32),
    )
    grad_picked = gates * (grad_gates - jnp.sum(gates * grad_gates, axis=-1, keepdims=True))
    grad_logits = jnp.einsum("tke,tk->te", choose, grad_picked, precision=PRECISE)
    grad_router = jnp.dot(normed2_wide.T, grad_logits, precision=PRECISE)
    grad_normed2 = grad_normed2 + jnp.dot(grad_logits, router_mat.T, precision=PRECISE)
    grad_mixed_part, grad_mid = norm_backward(grad_normed2, mid_vec, unit2, scaler2)
    grad_mixed = grad_final + grad_mixed_part
    grad_attn_low = grad_mixed.astype(jnp.bfloat16)
    grad_outproj = RESIDUAL_SCALE * jnp.dot(
        attended_low.T, grad_attn_low, preferred_element_type=jnp.float32
    )
    grad_attended = (
        RESIDUAL_SCALE * jnp.dot(grad_attn_low, out_full.T, preferred_element_type=jnp.float32)
    ).astype(jnp.bfloat16)
    grad_attended = grad_attended.reshape(seq_count, tok_count, KV_HEADS, head_groups, HEAD_DIM)
    keys_back, values_back = (
        lax.all_gather(key_low, "ctx", axis=1, tiled=True),
        lax.all_gather(value_low, "ctx", axis=1, tiled=True),
    )
    keys_split = keys_back.reshape(seq_count, SEQ_LEN, KV_HEADS, HEAD_DIM)
    values_back_split = values_back.reshape(seq_count, SEQ_LEN, KV_HEADS, HEAD_DIM)
    probs = jnp.exp(masked_scores(keys_back) - log_total)
    grad_probs = jnp.einsum(
        "sqjgd,skjd->sjgqk", grad_attended, values_back_split, preferred_element_type=jnp.float32
    )
    delta = jnp.sum(probs * grad_probs, axis=-1, keepdims=True)
    grad_scores_low = (probs * (grad_probs - delta)).astype(jnp.bfloat16)
    probs_back_low = probs.astype(jnp.bfloat16)
    grad_query_raw = (
        jnp.einsum(
            "sjgqk,skjd->sqjgd", grad_scores_low, keys_split, preferred_element_type=jnp.float32
        )
        * SCORE_SCALE
    )
    grad_query_rot = rotate(
        grad_query_raw.reshape(seq_count, tok_count, HEADS, HEAD_DIM),
        cosine_table,
        sine_table,
        -1.0,
    )
    grad_query_low = grad_query_rot.astype(jnp.bfloat16).reshape(row_count, HEADS * HEAD_DIM)
    row_total = tok_count * lax.axis_size("ctx")
    part_scores = lax.slice_in_dim(grad_scores_low, 0, row_total, axis=4)
    part_probs = lax.slice_in_dim(probs_back_low, 0, row_total, axis=4)
    term_keys = (
        jnp.einsum(
            "sjgqk,sqjgd->ksjd", part_scores, query_split, preferred_element_type=jnp.float32
        )
        * SCORE_SCALE
    )
    term_values = jnp.einsum(
        "sjgqk,sqjgd->ksjd", part_probs, grad_attended, preferred_element_type=jnp.float32
    )
    kv_summed = jnp.swapaxes(
        lax.psum_scatter(
            jnp.concatenate(
                [
                    term_keys.reshape(row_total, seq_count, kv_width),
                    term_values.reshape(row_total, seq_count, kv_width),
                ],
                -1,
            ).astype(jnp.bfloat16),
            "ctx",
            scatter_dimension=0,
            tiled=True,
        ).astype(jnp.float32),
        0,
        1,
    )
    grad_key_rot = rotate(
        kv_summed[..., :kv_width].reshape(seq_count, tok_count, KV_HEADS, HEAD_DIM),
        cosine_table,
        sine_table,
        -1.0,
    )
    grad_key_low = grad_key_rot.astype(jnp.bfloat16).reshape(row_count, kv_width)
    grad_value_low = kv_summed[..., kv_width:].astype(jnp.bfloat16).reshape(row_count, kv_width)
    grad_queryproj = jnp.dot(normed1_low.T, grad_query_low, preferred_element_type=jnp.float32)
    grad_keyproj = jnp.dot(normed1_low.T, grad_key_low, preferred_element_type=jnp.float32)
    grad_valueproj = jnp.dot(normed1_low.T, grad_value_low, preferred_element_type=jnp.float32)
    grad_normed1 = jnp.dot(grad_query_low, query_full.T, preferred_element_type=jnp.float32)
    grad_normed1 = grad_normed1 + jnp.dot(
        grad_key_low, key_full.T, preferred_element_type=jnp.float32
    )
    grad_normed1 = grad_normed1 + jnp.dot(
        grad_value_low, value_full.T, preferred_element_type=jnp.float32
    )
    grad_input_part, grad_pre = norm_backward(grad_normed1, pre_vec, unit1, scaler1)
    grad_input = (
        (grad_mixed + grad_input_part)
        .astype(jnp.bfloat16)
        .reshape(seq_count, tok_count, feature_dim)
    )
    weight_grads = (
        grad_pre,
        grad_queryproj,
        grad_keyproj,
        grad_valueproj,
        grad_outproj,
        grad_router,
        grad_mid,
    )
    weight_grads = (
        lax.psum(weight_grads[0].astype(jnp.bfloat16), "ctx").astype(jnp.float32),
        lax.psum(weight_grads[1].astype(jnp.bfloat16), "ctx").astype(jnp.float32),
        lax.psum(weight_grads[2].astype(jnp.bfloat16), "ctx").astype(jnp.float32),
        lax.psum(weight_grads[3].astype(jnp.bfloat16), "ctx").astype(jnp.float32),
        lax.psum(weight_grads[4].astype(jnp.bfloat16), "ctx").astype(jnp.float32),
        lax.psum(weight_grads[5].astype(jnp.bfloat16), "ctx").astype(jnp.float32),
        lax.psum(weight_grads[6].astype(jnp.bfloat16), "ctx").astype(jnp.float32),
    )
    shards = (
        lax.psum_scatter(
            weight_grads[0].astype(jnp.bfloat16), "fsdp", scatter_dimension=0, tiled=True
        ).astype(jnp.float32),
        lax.psum_scatter(
            weight_grads[1].astype(jnp.bfloat16), "fsdp", scatter_dimension=0, tiled=True
        ).astype(jnp.float32),
        lax.psum_scatter(
            weight_grads[2].astype(jnp.bfloat16), "fsdp", scatter_dimension=0, tiled=True
        ).astype(jnp.float32),
        lax.psum_scatter(
            weight_grads[3].astype(jnp.bfloat16), "fsdp", scatter_dimension=0, tiled=True
        ).astype(jnp.float32),
        lax.psum_scatter(
            weight_grads[4].astype(jnp.bfloat16), "fsdp", scatter_dimension=0, tiled=True
        ).astype(jnp.float32),
        lax.psum_scatter(
            weight_grads[5].astype(jnp.bfloat16), "fsdp", scatter_dimension=0, tiled=True
        ).astype(jnp.float32),
        lax.psum_scatter(
            weight_grads[6].astype(jnp.bfloat16), "fsdp", scatter_dimension=0, tiled=True
        ).astype(jnp.float32),
    )
    shard_pre, shard_query, shard_key, shard_value, shard_out, shard_router, shard_mid = shards
    shard_gate, shard_up, shard_down = expert_grads
    return (
        output,
        grad_input,
        shard_pre,
        shard_query,
        shard_key,
        shard_value,
        shard_out,
        shard_router,
        shard_mid,
        shard_gate,
        shard_up,
        shard_down,
    )


def solution(mesh):
    return jax.shard_map(
        on_device,
        mesh=mesh,
        in_specs=(
            P("fsdp", "ctx", None),
            P(),
            P("fsdp", "ctx", None),
            P("fsdp"),
            P("fsdp", None),
            P("fsdp", None),
            P("fsdp", None),
            P("fsdp", None),
            P("fsdp", None),
            P("fsdp"),
            P("ctx", "fsdp", None),
            P("ctx", "fsdp", None),
            P("ctx", "fsdp", None),
            P("fsdp", "ctx", None),
        ),
        out_specs=(
            P("fsdp", "ctx", None),
            P("fsdp", "ctx", None),
            P("fsdp"),
            P("fsdp", None),
            P("fsdp", None),
            P("fsdp", None),
            P("fsdp", None),
            P("fsdp", None),
            P("fsdp"),
            P("ctx", "fsdp", None),
            P("ctx", "fsdp", None),
            P("ctx", "fsdp", None),
        ),
        check_vma=False,
    )
```

profile of v0, /device:TPU:17, one launch (start us, length us, event | category | flops | bytes accessed | tf_op | source)
XLA Modules:
  0.0 1469.6 jit_solution(14862182575506526253)
XLA Ops:
  12.4 22.8 %all-reduce.5 = (bf16[1536]{0:T(1024)(128)(2,1)S(1)}, bf16[1536]{0:T(1024)(128)(2,1)S(1)}) all-reduce(bf16[1536]{0:T(1024)(128)(2,1)S(1)} %dynamic-update-slice.3, bf16[1536]{0:T(1024)(128)(2,1)S(1)} %dynamic-update-slice.4), channel_id=1, replica_groups=mesh['ctx'=8,'fsdp'=16] {'fsdp'}, use_global_device_ids=true, to_apply=%add | all-reduce | flops 3072 | bytes 12288
  59.9 19.9 %all-gather.15.cloned.1.call-done = bf16[1536,512]{1,0:T(8,128)(2,1)} async-done(((bf16[96,512]{1,0:T(8,128)(2,1)}), bf16[1536,512]{1,0:T(8,128)(2,1)}) %all-gather.15.cloned.1.call-update) | async-done | bytes 1572880 | tf_op jit(solution)/shard_map/all_gather | solution.py:77
  111.3 15.7 %all-gather.2 = bf16[16,96,40]{1,2,0:T(8,128)(2,1)S(1)} all-gather(bf16[1,96,40]{1,2,0:T(8,128)(2,1)S(1)} %bitcast.371), channel_id=1, replica_groups=mesh['ctx'=8,'fsdp'=16] {'fsdp'}, dimensions={0}, use_global_device_ids=true | all-gather | bytes 130560 | tf_op jit(solution)/shard_map/all_gather | solution.py:80
  132.4 47.2 %all-gather.29.cloned.1.call-done = bf16[1024,512]{1,0:T(8,128)(2,1)} async-done(((bf16[128,512]{1,0:T(8,128)(2,1)}), bf16[1024,512]{1,0:T(8,128)(2,1)}) %all-gather.29.cloned.1.call-update) | async-done | bytes 1048592 | tf_op jit(solution)/shard_map/all_gather | solution.py:112
  181.0 37.7 %all-gather.17.cloned.1.call-done = bf16[1536,1536]{1,0:T(8,128)(2,1)} async-done(((bf16[96,1536]{1,0:T(8,128)(2,1)}), bf16[1536,1536]{1,0:T(8,128)(2,1)}) %all-gather.17.cloned.1.call-update) | async-done | bytes 4718608 | tf_op jit(solution)/shard_map/all_gather | solution.py:76
  232.5 26.4 %all-gather.19.cloned.1.call-done = bf16[1536,1536]{1,0:T(8,128)(2,1)} async-done(((bf16[96,1536]{1,0:T(8,128)(2,1)}), bf16[1536,1536]{1,0:T(8,128)(2,1)}) %all-gather.19.cloned.1.call-update) | async-done | bytes 4718608 | tf_op jit(solution)/shard_map/all_gather | solution.py:79
  283.4 54.9 %all_to_all.20 = bf16[5,8,32,1536]{3,2,0,1:T(8,128)(2,1)} all-to-all(bf16[5,8,32,1536]{3,2,0,1:T(8,128)(2,1)S(1)} %get-tuple-element.73), channel_id=1, replica_groups=mesh['ctx'=8,'fsdp'=16] {'ctx'}, dimensions={1} | all-to-all | bytes 7864320 | tf_op jit(solution)/shard_map/all_to_all | solution.py:208
  347.4 43.8 %all-to-all-done = bf16[5,8,32,1536]{3,2,0,1:T(8,128)(2,1)} async-done(((bf16[5,8,32,1536]{3,2,0,1:T(8,128)(2,1)}), bf16[5,8,32,1536]{3,2,0,1:T(8,128)(2,1)}, u32[]{:S(2)}, u32[]{:S(2)}) %all-to-all-start) | async-done | bytes 3932192 | tf_op jit(solution)/shard_map/all_to_all | solution.py:168
  403.7 28.4 %all-gather.21.cloned.1.call-done = bf16[5,1536,512]{2,1,0:T(8,128)(2,1)} async-done(((bf16[5,96,512]{2,1,0:T(8,128)(2,1)}), bf16[5,1536,512]{2,1,0:T(8,128)(2,1)}) %all-gather.21.cloned.1.call-update) | async-done | bytes 7864336 | tf_op jit(solution)/shard_map/all_gather | solution.py:172
  440.2 45.9 %all-gather.25.cloned.1.call-done = bf16[5,512,1536]{2,1,0:T(8,128)(2,1)} async-done(((bf16[5,32,1536]{2,1,0:T(8,128)(2,1)}), bf16[5,512,1536]{2,1,0:T(8,128)(2,1)}) %all-gather.25.cloned.1.call-update) | async-done | bytes 7864336 | tf_op jit(solution)/shard_map/all_gather | solution.py:174
  525.1 30.3 %all-to-all-done.1 = bf16[5,8,32,1536]{3,2,0,1:T(8,128)(2,1)} async-done(((bf16[5,8,32,1536]{3,2,0,1:T(8,128)(2,1)}), bf16[5,8,32,1536]{3,2,0,1:T(8,128)(2,1)}, u32[]{:S(2)}, u32[]{:S(2)}) %all-to-all-start.1) | async-done | bytes 3932192 | tf_op jit(solution)/shard_map/all_to_all | solution.py:184
  591.3 27.9 %all-to-all-done.3 = bf16[5,8,32,1536]{3,2,0,1:T(8,128)(2,1)} async-done(((bf16[5,8,32,1536]{3,2,0,1:T(8,128)(2,1)}), bf16[5,8,32,1536]{3,2,0,1:T(8,128)(2,1)}, u32[]{:S(2)}, u32[]{:S(2)}) %all-to-all-start.3) | async-done | bytes 3932192 | tf_op jit(solution)/shard_map/all_to_all | solution.py:234
  673.8 82.1 %reduce-scatter.28.cloned.1.call-done = bf16[128,1024]{1,0:T(8,128)(2,1)} async-done(((bf16[1024,1024]{1,0:T(8,128)(2,1)}), bf16[128,1024]{1,0:T(8,128)(2,1)}) %reduce-scatter.28.cloned.1.call-update) | async-done | bytes 262160
  777.8 32.5 %reduce-scatter.24.cloned.1.call-done = bf16[96,512]{1,0:T(8,128)(2,1)} async-done(((bf16[1536,512]{1,0:T(8,128)(2,1)}), bf16[96,512]{1,0:T(8,128)(2,1)}) %reduce-scatter.24.cloned.1.call-update) | async-done | bytes 98320 | tf_op jit(solution)/shard_map/reduce_scatter | solution.py:378
  810.2 63.5 %reduce-scatter.22.cloned.1.call-done = bf16[96,512]{1,0:T(8,128)(2,1)} async-done(((bf16[1536,512]{1,0:T(8,128)(2,1)}), bf16[96,512]{1,0:T(8,128)(2,1)}) %reduce-scatter.22.cloned.1.call-update) | async-done | bytes 98320 | tf_op jit(solution)/shard_map/reduce_scatter | solution.py:375
  873.7 77.7 %reduce-scatter.26.cloned.1.call-done = bf16[96,1536]{1,0:T(8,128)(2,1)} async-done(((bf16[1536,1536]{1,0:T(8,128)(2,1)}), bf16[96,1536]{1,0:T(8,128)(2,1)}) %reduce-scatter.26.cloned.1.call-update) | async-done | bytes 294928 | tf_op jit(solution)/shard_map/reduce_scatter | solution.py:381
  951.5 70.3 %reduce-scatter.20.cloned.1.call-done = bf16[96,1536]{1,0:T(8,128)(2,1)} async-done(((bf16[1536,1536]{1,0:T(8,128)(2,1)}), bf16[96,1536]{1,0:T(8,128)(2,1)}) %reduce-scatter.20.cloned.1.call-update) | async-done | bytes 294928 | tf_op jit(solution)/shard_map/reduce_scatter | solution.py:372
  1053.4 23.3 %reduce-scatter.30.cloned.1.call-done = bf16[96,40]{1,0:T(8,128)(2,1)} async-done(((bf16[1536,40]{1,0:T(8,128)(2,1)}), bf16[96,40]{1,0:T(8,128)(2,1)}) %reduce-scatter.30.cloned.1.call-update) | async-done | bytes 7696
  1080.3 27.6 %all-reduce.4 = (bf16[1536]{0:T(1024)(128)(2,1)S(1)}, bf16[1536]{0:T(1024)(128)(2,1)S(1)}) all-reduce(bf16[1536]{0:T(1024)(128)(2,1)S(1)} %get-tuple-element.28, bf16[1536]{0:T(1024)(128)(2,1)S(1)} %get-tuple-element.26), channel_id=5, replica_groups=mesh['ctx'=8,'fsdp'=16] {'fsdp'}, use_global_device_ids=true, to_apply=%region_21.22.clone | all-reduce | flops 3072 | bytes 12288
  1108.1 34.6 %all-reduce.6 = (bf16[96]{0:T(256)(128)(2,1)S(1)}, bf16[96,40]{0,1:T(8,128)(2,1)S(1)}, bf16[96]{0:T(256)(128)(2,1)S(1)}) all-reduce(bf16[96]{0:T(256)(128)(2,1)S(1)} %dynamic-slice.9, bf16[96,40]{0,1:T(8,128)(2,1)S(1)} %copy.159, bf16[96]{0:T(256)(128)(2,1)S(1)} %dynamic-slice.11), channel_id=1, replica_groups=mesh['ctx'=8,'fsdp'=16] {'ctx'}, use_global_device_ids=true, to_apply=%region_20.21 | all-reduce | flops 4032 | bytes 16128 | tf_op jit(solution)/shard_map/psum | solution.py:360
  1145.4 25.5 %all-reduce.10.cloned.1.call-done = (bf16[96,1536]{1,0:T(8,128)(2,1)}, bf16[96,512]{1,0:T(8,128)(2,1)}, bf16[96,512]{1,0:T(8,128)(2,1)}, bf16[96,1536]{1,0:T(8,128)(2,1)}) async-done(((bf16[96,1536]{1,0:T(8,128)(2,1)}, bf16[96,512]{1,0:T(8,128)(2,1)}, bf16[96,512]{1,0:T(8,128)(2,1)}, bf16[96,1536]{1,0:T(8,128)(2,1)}), (bf16[96,1536]{1,0:T(8,128)(2,1)}, bf16[96,512]{1,0:T(8,128)(2,1)}, ...) | async-done | bytes 786448 | tf_op jit(solution)/shard_map/psum | solution.py:361
  1177.7 91.7 %reduce-scatter.18.cloned.1.call-done = bf16[5,32,1536]{2,1,0:T(8,128)(2,1)} async-done(((bf16[5,512,1536]{2,1,0:T(8,128)(2,1)}), bf16[5,32,1536]{2,1,0:T(8,128)(2,1)}) %reduce-scatter.18.cloned.1.call-update) | async-done | bytes 491536 | tf_op jit(solution)/shard_map/reduce_scatter | solution.py:254
  1271.5 93.4 %reduce-scatter.16.cloned.1.call-done = bf16[5,96,512]{2,1,0:T(8,128)(2,1)} async-done(((bf16[5,1536,512]{2,1,0:T(8,128)(2,1)}), bf16[5,96,512]{2,1,0:T(8,128)(2,1)}) %reduce-scatter.16.cloned.1.call-update) | async-done | bytes 491536 | tf_op jit(solution)/shard_map/reduce_scatter | solution.py:251
  1367.0 93.6 %reduce-scatter.14.cloned.1.call-done = bf16[5,96,512]{2,1,0:T(8,128)(2,1)} async-done(((bf16[5,1536,512]{2,1,0:T(8,128)(2,1)}), bf16[5,96,512]{2,1,0:T(8,128)(2,1)}) %reduce-scatter.14.cloned.1.call-update) | async-done | bytes 491536 | tf_op jit(solution)/shard_map/reduce_scatter | solution.py:248
  (323 shorter events, 335.9 us)
Async XLA Ops:
  7.2 37.7 %all-gather.13.cloned.1.call-start = ((), (), s32[]{:S(2)}) async-start(), calls=%async_computation.13 | async-start | bytes 1671168 | tf_op jit(solution)/shard_map/all_gather | solution.py:78
  7.9 71.8 %all-gather.15.cloned.1.call-start = ((), (), s32[]{:S(2)}) async-start(), calls=%async_computation.14 | async-start | bytes 1671168 | tf_op jit(solution)/shard_map/all_gather | solution.py:77
  8.7 122.0 %all-gather.27.cloned.1.call-start = ((), (), s32[]{:S(2)}) async-start(), calls=%async_computation.23 | async-start | bytes 1179648 | tf_op jit(solution)/shard_map/all_gather | solution.py:113
  35.3 183.4 %copy-start.37 = (f32[1536]{0:T(1024)}, f32[1536]{0:T(1024)S(1)}, u32[]{:S(2)}) copy-start(f32[1536]{0:T(1024)S(1)} %convert_element_type.250) | copy-start | bytes 18436
  47.5 132.0 %all-gather.29.cloned.1.call-start = ((), (), s32[]{:S(2)}) async-start(), calls=%async_computation.24 | async-start | bytes 1179648 | tf_op jit(solution)/shard_map/all_gather | solution.py:112
  82.7 136.0 %all-gather.17.cloned.1.call-start = ((), (), s32[]{:S(2)}) async-start(), calls=%async_computation.15 | async-start | bytes 5013504 | tf_op jit(solution)/shard_map/all_gather | solution.py:76
  83.3 175.6 %all-gather.19.cloned.1.call-start = ((), (), s32[]{:S(2)}) async-start(), calls=%async_computation.16 | async-start | bytes 5013504 | tf_op jit(solution)/shard_map/all_gather | solution.py:79
  83.9 311.7 %all-gather.23.cloned.1.call-start = ((), (), s32[]{:S(2)}) async-start(), calls=%async_computation.18 | async-start | bytes 8355840 | tf_op jit(solution)/shard_map/all_gather | solution.py:173
  84.6 347.5 %all-gather.21.cloned.1.call-start = ((), (), s32[]{:S(2)}) async-start(), calls=%async_computation.17 | async-start | bytes 8355840 | tf_op jit(solution)/shard_map/all_gather | solution.py:172
  85.4 400.8 %all-gather.25.cloned.1.call-start = ((), (), s32[]{:S(2)}) async-start(), calls=%async_computation.19 | async-start | bytes 8355840 | tf_op jit(solution)/shard_map/all_gather | solution.py:174
  338.3 52.8 %all-to-all-start = ((bf16[5,8,32,1536]{3,2,0,1:T(8,128)(2,1)}), bf16[5,8,32,1536]{3,2,0,1:T(8,128)(2,1)}, u32[]{:S(2)}, u32[]{:S(2)}) async-start(bf16[5,8,32,1536]{3,2,0,1:T(8,128)(2,1)} %get-tuple-element.74), calls=%async_computation | async-start | bytes 7864320 | tf_op jit(solution)/shard_map/all_to_all | solution.py:168
  500.5 54.9 %all-to-all-start.1 = ((bf16[5,8,32,1536]{3,2,0,1:T(8,128)(2,1)}), bf16[5,8,32,1536]{3,2,0,1:T(8,128)(2,1)}, u32[]{:S(2)}, u32[]{:S(2)}) async-start(bf16[5,8,32,1536]{3,2,0,1:T(8,128)(2,1)} %copy.127), calls=%async_computation.1 | async-start | bytes 7864320 | tf_op jit(solution)/shard_map/all_to_all | solution.py:184
  555.4 63.8 %all-to-all-start.3 = ((bf16[5,8,32,1536]{3,2,0,1:T(8,128)(2,1)}), bf16[5,8,32,1536]{3,2,0,1:T(8,128)(2,1)}, u32[]{:S(2)}, u32[]{:S(2)}) async-start(bf16[5,8,32,1536]{3,2,0,1:T(8,128)(2,1)} %copy.131), calls=%async_computation.3 | async-start | bytes 7864320 | tf_op jit(solution)/shard_map/all_to_all | solution.py:234
  570.9 185.0 %reduce-scatter.28.cloned.1.call-start = ((), (), s32[]{:S(2)}) async-start(), calls=%async_computation.29 | async-start | bytes 2359296
  673.8 136.5 %reduce-scatter.24.cloned.1.call-start = ((), (), s32[]{:S(2)}) async-start(), calls=%async_computation.27 | async-start | bytes 1671168 | tf_op jit(solution)/shard_map/reduce_scatter | solution.py:378
  758.9 114.8 %reduce-scatter.22.cloned.1.call-start = ((), (), s32[]{:S(2)}) async-start(), calls=%async_computation.26 | async-start | bytes 1671168 | tf_op jit(solution)/shard_map/reduce_scatter | solution.py:375
  761.1 190.4 %reduce-scatter.26.cloned.1.call-start = ((), (), s32[]{:S(2)}) async-start(), calls=%async_computation.28 | async-start | bytes 5013504 | tf_op jit(solution)/shard_map/reduce_scatter | solution.py:381
  764.8 257.0 %reduce-scatter.20.cloned.1.call-start = ((), (), s32[]{:S(2)}) async-start(), calls=%async_computation.25 | async-start | bytes 5013504 | tf_op jit(solution)/shard_map/reduce_scatter | solution.py:372
  775.6 246.3 %copy-start.10 = (bf16[5,256,512]{2,1,0:T(8,128)(2,1)S(1)}, bf16[5,256,512]{2,1,0:T(8,128)(2,1)}, u32[]{:S(2)}) copy-start(bf16[5,256,512]{2,1,0:T(8,128)(2,1)} %copy-done.9) | copy-start | bytes 3932164
  775.6 301.1 %reduce-scatter.30.cloned.1.call-start = ((), (), s32[]{:S(2)}) async-start(), calls=%async_computation.30 | async-start | bytes 417792
  777.7 393.2 %all-reduce.10.cloned.1.call-start = ((), (), s32[]{:S(2)}) async-start(), calls=%async_computation.31 | async-start | bytes 1572864 | tf_op jit(solution)/shard_map/psum | solution.py:361
  1021.8 247.6 %reduce-scatter.18.cloned.1.call-start = ((), (), s32[]{:S(2)}) async-start(), calls=%async_computation.22 | async-start | bytes 8355840 | tf_op jit(solution)/shard_map/reduce_scatter | solution.py:254
  1029.3 335.6 %reduce-scatter.16.cloned.1.call-start = ((), (), s32[]{:S(2)}) async-start(), calls=%async_computation.21 | async-start | bytes 8355840 | tf_op jit(solution)/shard_map/reduce_scatter | solution.py:251
  1038.1 422.5 %reduce-scatter.14.cloned.1.call-start = ((), (), s32[]{:S(2)}) async-start(), calls=%async_computation.20 | async-start | bytes 8355840 | tf_op jit(solution)/shard_map/reduce_scatter | solution.py:248
  (59 other events, 1959.7 us)
Sparse Core Ops, SparseCore 0:
  9.7 35.0 all-gather.12
  46.5 33.1 all-gather.14
  82.7 47.9 all-gather.26
  133.4 46.0 all-gather.28
  181.1 37.5 all-gather.16
  220.3 38.5 all-gather.18
  260.5 91.3 all-gather.22
  353.6 78.4 all-gather.20
  433.8 52.2 all-gather.24
  673.9 81.9 reduce-scatter.27
  759.0 51.1 reduce-scatter.23
  812.5 61.2 reduce-scatter.21
  876.3 75.1 reduce-scatter.25
  953.9 67.8 reduce-scatter.19
  1024.7 52.0 reduce-scatter.29
  1079.3 91.5 all-reduce.9
  1173.3 96.0 reduce-scatter.17
  1271.8 93.0 reduce-scatter.15
  1367.4 93.0 reduce-scatter.13
where the time goes:
time: 1480 us; the launch traced here: 1470 us
  waiting for transfers between devices  973 us (66%)
  blocking collectives  156 us (11%)
  matrix products  128 us (9%)
  local copies, waits for them, and re-layouts  97.4 us (7%)
  other arithmetic  70.4 us (5%)
  starting transfers between devices  27.6 us (2%)
  between operations  17.1 us (1%)
    unnamed x21, waiting for transfers between devices  110 us
    reduce_scatter x1, waiting for transfers between devices, on_device(): lax.psum_scatter(grad_gate_full.astype(jnp.bfloat16), 'fsdp', scatter_dim...  93.6 us
    reduce_scatter x1, waiting for transfers between devices, on_device(): lax.psum_scatter(grad_up_full.astype(jnp.bfloat16), 'fsdp', scatter_dimen...  93.4 us
    reduce_scatter x1, waiting for transfers between devices, on_device(): lax.psum_scatter(grad_down_full.astype(jnp.bfloat16), 'fsdp', scatter_dim...  91.7 us
    reduce_scatter x1, waiting for transfers between devices, on_device(): lax.psum_scatter(weight_grads[4].astype(jnp.bfloat16), 'fsdp', scatter_di...  77.7 us
    reduce_scatter x1, waiting for transfers between devices, on_device(): lax.psum_scatter(weight_grads[1].astype(jnp.bfloat16), 'fsdp', scatter_di...  70.3 us
    reduce_scatter x1, waiting for transfers between devices, on_device(): lax.psum_scatter(weight_grads[2].astype(jnp.bfloat16), 'fsdp', scatter_di...  63.5 us
    all_to_all x1, blocking collectives, on_device(): lax.all_to_all(grad_send, 'ctx', split_axis=1, concat_axis=1, tiled=True)  54.9 us
  transfers between devices with their start and end apart: 22, of which 21 were waited for; matrix products, arithmetic and copies ran while one was open for 14% of the time, Pallas kernels for 0%

commit v1 on v0

v1 whole, which is shorter than its diff:
```python
import functools
import jax
import jax.numpy as jnp
from jax import lax
from jax.experimental import pallas as pl
from jax.experimental.pallas import tpu as pltpu
from jax.sharding import PartitionSpec as P

D = 1536
HEADS = 24
KV_HEADS = 8
HEAD_DIM = 64
FF = 512
EXPERTS = 40
TOP = 8
SEQ_LEN = 1024
TOK = 128
MOST = 32
N_CTX = 8
LOCAL = EXPERTS // N_CTX
SLOTS = N_CTX * MOST
ROWS = LOCAL * MOST
QW = HEADS * HEAD_DIM // N_CTX
EPSILON = 1e-06
SCORE_SCALE = 0.015625
RES = 0.22
THETA_BASE = 10000.0
BF = jnp.bfloat16
F32 = jnp.float32
MIB = 1 << 20

NT = (((1,), (1,)), ((), ()))
TN = (((0,), (0,)), ((), ()))


def dot(a, b):
    return jnp.dot(a, b, preferred_element_type=F32)


def dotg(a, b, dims):
    return lax.dot_general(a, b, dims, preferred_element_type=F32)


def ctx_pairs(dr, dp):
    return [(z * 4 + x, (z ^ dp) * 4 + (x + dr) % 4) for z in range(2) for x in range(4)]


def fsdp_pairs(dr, dp, dc):
    return [
        (y * 4 + z * 2 + c, ((y + dr) % 4) * 4 + (z ^ dp) * 2 + (c ^ dc))
        for y in range(4)
        for z in range(2)
        for c in range(2)
    ]


def cs(v, dr, dp=0):
    return lax.ppermute(v, "ctx", ctx_pairs(dr, dp))


def fs(v, dr, dp=0, dc=0):
    return lax.ppermute(v, "fsdp", fsdp_pairs(dr, dp, dc))


def gather2(s, send):
    left = send(s, 1)
    right = send(s, -1)
    pair = send(s, 0, 1)
    return [s, right, send(s, 2), left, pair, send(pair, -1), send(pair, 2), send(pair, 1)]


def add_low(a, *rest):
    total = a.astype(F32)
    for r in rest:
        total = total + r.astype(F32)
    return total.astype(BF)


def scatter2_parts(blocks, send):
    b1 = send(blocks[5], 1)
    b2 = send(blocks[6], 2)
    b3 = send(blocks[7], -1)
    a1 = send(blocks[1], 1)
    a2 = send(blocks[2], 2)
    a3 = send(blocks[3], -1)
    p = send(add_low(blocks[4], b1, b2, b3), 0, 1)
    return [blocks[0], a1, a2, a3, p]


def after(v, *done):
    return lax.optimization_barrier((v,) + done)[0]


def halves(v):
    n = v.shape[0] // 2
    return v[:n], v[n:]


def gather3(s, send):
    L = send(s, 1)
    R = send(s, -1)
    Q = send(s, 0, 1)
    L1, L2 = halves(L)
    R1, R2 = halves(R)
    Q1, Q2 = halves(Q)
    A = jnp.concatenate([send(L1, 1), send(R2, -1)])
    QL = jnp.concatenate([send(Q1, 1), send(L2, 0, 1)])
    QR = jnp.concatenate([send(Q1, -1), send(R2, 0, 1)])
    n = s.shape[0] // 3
    QA = jnp.concatenate([send(A[:n], 0, 1), send(QL[n : 2 * n], 1), send(QR[2 * n :], -1)])
    return [s, R, A, L, Q, QR, QA, QL]


def scatter3_first(QA, send):
    n = QA.shape[0] // 3
    return send(QA[:n], 0, 1), send(QA[n : 2 * n], 1), send(QA[2 * n :], -1)


def scatter3_second(A, QR, QL, firsts):
    n = A[0].shape[0] // 3
    g1, g2, g3 = firsts
    cut = lambda v, lo, hi, *more: add_low(v[0][lo:hi], v[1][lo:hi], *more)
    A = jnp.concatenate([cut(A, 0, n, g1), cut(A, n, 3 * n)])
    QR = jnp.concatenate([cut(QR, 0, n), cut(QR, n, 2 * n, g2), cut(QR, 2 * n, 3 * n)])
    QL = jnp.concatenate([cut(QL, 0, 2 * n), cut(QL, 2 * n, 3 * n, g3)])
    return halves(A) + halves(QR) + halves(QL)


def scatter3_send(ops, send):
    A1, A2, R1, R2, L1, L2 = ops
    return (
        send(A1, 1),
        send(R1, 1),
        send(A2, -1),
        send(L1, -1),
        send(R2, 0, 1),
        send(L2, 0, 1),
    )


def scatter3_third(R, L, Q, seconds):
    a1, r1, a2, l1, r2, l2 = seconds
    h, n = a1.shape[0], R[0].shape[0]
    cut = lambda v, lo, hi, *more: add_low(v[0][lo:hi], v[1][lo:hi], *more)
    R = jnp.concatenate([cut(R, 0, h, a1), cut(R, h, n, r2)])
    L = jnp.concatenate([cut(L, 0, h), cut(L, h, n, a2, l2)])
    Q = jnp.concatenate([cut(Q, 0, h, r1, l1), cut(Q, h, n)])
    return R, L, Q


def specs(n):
    return [pl.BlockSpec(memory_space=pltpu.VMEM)] * n


SM = pl.BlockSpec(memory_space=pltpu.SMEM)
HB = pl.BlockSpec(memory_space=pl.ANY)


OUT_BLOCK = pl.BlockSpec((D, D), lambda i: (0, 0))
QKV_BLOCK = pl.BlockSpec((D, 384), lambda i: (0, 4))
X_BLOCK = pl.BlockSpec((TOK, D), lambda i: (0, 0))


def sds(shape, dtype):
    return jax.ShapeDtypeStruct(shape, dtype)


def lane(shape):
    return lax.broadcasted_iota(jnp.int32, shape, 1)


def swap32(v):
    w = v.shape[1]
    up = pltpu.roll(v, w - 32, 1)
    down = pltpu.roll(v, 32, 1)
    return jnp.where(lane(v.shape) % 64 < 32, up, down)


def params(mib=56):
    return pltpu.CompilerParams(vmem_limit_bytes=mib * MIB)


def cost(flops, nbytes):
    return pl.CostEstimate(flops=int(flops), bytes_accessed=int(nbytes), transcendentals=0)


def attn_fwd_kernel(order, *refs):
    xs = refs[:8]
    w, gain, cosb, sinb, posq, posk = refs[8:14]
    h1, qkv, o, lse, kk, vv = refs[14:]
    lo = lane((TOK, 128)) < 64
    for k in range(8):
        b = order[k]
        rows = pl.ds(pl.multiple_of(b * TOK, TOK), TOK)
        x = xs[k][...].astype(F32)
        scaler = lax.rsqrt(jnp.mean(x * x, axis=-1, keepdims=True) + EPSILON)
        h = (x * scaler * gain[...]).astype(BF)
        h1[rows, :] = h
        raw = dot(h, w[...])
        qk = raw[:, :256]
        cos = cosb[rows, :]
        sin = sinb[rows, :]
        cos2 = jnp.concatenate([cos, cos], axis=1)
        sin2 = jnp.concatenate([sin, sin], axis=1)
        rot = qk * cos2 + swap32(qk) * sin2
        t2 = jnp.where(lo, raw[:, 256:], 0.0)
        qkv[rows, :256] = rot.astype(BF)
        qkv[rows, 256:] = t2.astype(BF)
        t1 = rot[:, 128:]
        kk[rows, :] = jnp.where(lo, pltpu.roll(t1, 64, 1), t1).astype(BF)
        vv[rows, :] = (t2 + pltpu.roll(t2, 64, 1)).astype(BF)

    def block(b, carry):
        rows = pl.ds(pl.multiple_of(b * TOK, TOK), TOK)
        vis = posk[...] <= posq[rows, :]
        t0 = qkv[rows, :128]
        t1 = qkv[rows, 128:256]
        zero = jnp.zeros_like(t0)
        outs = []
        logs = []
        for q in (jnp.where(lo, t0, zero), jnp.where(lo, zero, t0), jnp.where(lo, t1, zero)):
            s = dotg(q, kk[...], NT) * SCORE_SCALE
            s = jnp.where(vis, s, -1e30)
            top = jnp.max(s, axis=-1, keepdims=True)
            e = jnp.exp(s - top)
            total = jnp.sum(e, axis=-1, keepdims=True)
            p = (e * (1.0 / total)).astype(BF)
            outs.append(dot(p, vv[...]))
            logs.append(top + jnp.log(total))
        o[b, :, :128] = jnp.where(lo, outs[0], outs[1]).astype(BF)
        o[b, :, 128:] = jnp.where(lo, outs[2], 0.0).astype(BF)
        ln = lane((TOK, 128))
        lse[rows, :] = jnp.where(ln == 0, logs[0], jnp.where(ln == 1, logs[1], logs[2]))
        return carry

    lax.fori_loop(0, 8, block, 0)


def attn_fwd(order, xs, w, gain, cosb, sinb, posq, posk):
    return pl.pallas_call(
        attn_fwd_kernel,
        grid=(1,),
        out_shape=(
            sds((SEQ_LEN, D), BF),
            sds((SEQ_LEN, 384), BF),
            sds((8, TOK, 256), BF),
            sds((SEQ_LEN, 128), F32),
        ),
        in_specs=[SM] + [X_BLOCK] * 8 + [QKV_BLOCK] + specs(5),
        out_specs=tuple(specs(4)),
        scratch_shapes=[pltpu.VMEM((SEQ_LEN, 128), BF), pltpu.VMEM((SEQ_LEN, 128), BF)],
        compiler_params=params(),
        cost_estimate=cost(6e9, 12e6),
        name="attn_fwd",
    )(order, *xs, w, gain, cosb, sinb, posq, posk)


def out_proj_kernel(oa, w_out, x, gain, x2, h2, oc):
    o = jnp.concatenate([oa[s, :, :QW] for s in range(8)], axis=1)
    oc[...] = o
    v = x[...].astype(F32) + RES * dot(o, w_out[...])
    x2[...] = v
    scaler = lax.rsqrt(jnp.mean(v * v, axis=-1, keepdims=True) + EPSILON)
    h2[...] = (v * scaler * gain[...]).astype(BF)


def out_proj(oa, w_out, x, gain):
    return pl.pallas_call(
        out_proj_kernel,
        grid=(1,),
        out_shape=(sds((TOK, D), F32), sds((TOK, D), BF), sds((TOK, D), BF)),
        in_specs=specs(1) + [OUT_BLOCK] + specs(2),
        out_specs=tuple(specs(3)),
        compiler_params=params(),
        cost_estimate=cost(3e9, 8e6),
        name="out_proj",
    )(oa, w_out, x, gain)


def experts_kernel(order, first, *refs):
    h2s = refs[:8]
    xs = refs[8:16]
    wr, pieces, pieces3 = refs[16:19]
    xo, dro, uo, dao, dbo = refs[19:24]
    dhs, yall = refs[24:32], refs[32]
    wg, wu, wd, hbuf, gbuf, rg, dx, pds, gsl = refs[33:42]
    wsem, isem, osem = refs[42:]
    loads = []
    for k in range(8):
        loads.append(pltpu.make_async_copy(h2s[k], hbuf.at[k, :, pl.ds(0, D)], isem.at[0, k]))
        loads.append(pltpu.make_async_copy(xs[k].at[:, pl.ds(D, D + 128)], gbuf.at[k], isem.at[1, k]))
    for c in loads:
        c.start()
    wloads = []
    for k in range(16):
        r96 = pl.ds(k * 96, 96)
        r32 = pl.ds(k * 32, 32)
        for j, (src, dest) in enumerate(
            (
                (pieces.at[k, pl.ds(0, 5)], wg.at[:, r96, :]),
                (pieces.at[k, pl.ds(5, 5)], wu.at[:, r96, :]),
                (pieces3.at[k, pl.ds(10, 5)], wd.at[:, :, r32, :]),
            )
        ):
            wloads.append(pltpu.make_async_copy(src, dest, wsem.at[j, k]))
    for c in wloads:
        c.start()
    start = first[0]
    rowi = lax.broadcasted_iota(jnp.int32, (48, TOK), 0)
    upper = (
        lax.broadcasted_iota(jnp.int32, (TOK, TOK), 0)
        <= lax.broadcasted_iota(jnp.int32, (TOK, TOK), 1)
    ).astype(BF)
    slot = lax.broadcasted_iota(jnp.int32, (MOST, TOK), 0).astype(F32) + 1.0
    for k in range(8):
        loads[2 * k].wait()
        loads[2 * k + 1].wait()
        rt = jnp.transpose(gbuf[k, :, D:].astype(F32)).astype(jnp.int32) - start
        rt = jnp.where(rt < 0, rt + EXPERTS, rt)
        member = rowi == rt[0:1, :]
        for j in range(1, TOP):
            member = member | (rowi == rt[j : j + 1, :])
        mask = jnp.where(member, 1.0, 0.0)
        h = hbuf[k, :, :D]
        logits = jnp.where(member, dotg(wr[...], h, NT), -1e30)
        e = jnp.exp(logits - jnp.max(logits, axis=0, keepdims=True)) * mask
        gates = e / jnp.sum(e, axis=0, keepdims=True)
        rank = dot(mask.astype(BF), upper)
        sel = [
            jnp.where((slot == rank[i : i + 1, :]) & (mask[i : i + 1, :] > 0.0), 1.0, 0.0)
            for i in range(LOCAL)
        ]
        pd = jnp.concatenate(sel, axis=0).astype(BF)
        pds[k] = pd
        xb = dot(pd, h).astype(BF)
        gb = dot(pd, gbuf[k, :, :D]).astype(BF)
        for i in range(LOCAL):
            xo[i, k * MOST : (k + 1) * MOST, :] = xb[i * MOST : (i + 1) * MOST]
            dro[i, k * MOST : (k + 1) * MOST, :] = gb[i * MOST : (i + 1) * MOST]
            gcol = jnp.sum(sel[i] * gates[i : i + 1, :], axis=1, keepdims=True)
            gsl[i, k * MOST : (k + 1) * MOST, :] = jnp.broadcast_to(gcol, (MOST, 128))
    for c in wloads:
        c.wait()

    def expert(i, carry):
        x = xo[i]
        a = dot(x, wg[i])
        b = dot(x, wu[i])
        sig = jax.nn.sigmoid(a)
        act = a * sig
        u = (act * b).astype(BF)
        uo[i] = u
        gcol = gsl[i][:, 0:1]
        at = pl.ds(pl.multiple_of(i * MOST, MOST), MOST)
        du = jnp.zeros((SLOTS, FF), F32)
        dsum = jnp.zeros((SLOTS, 1), F32)
        for j in range(3):
            cols = slice(j * FF, (j + 1) * FF)
            r = dot(u, wd[i, j]).astype(BF).astype(F32)
            gj = dro[i, :, cols].astype(F32)
            dsum = dsum + jnp.sum(r * gj, axis=1, keepdims=True)
            rgj = (r * gcol).astype(BF)
            for k in range(8):
                rg[k, at, cols] = rgj[k * MOST : (k + 1) * MOST]
            drj = ((RES * gcol) * gj).astype(BF)
            dro[i, :, cols] = drj
            du = du + dotg(drj, wd[i, j], NT)
        da = (du * b * sig * (1.0 + a * (1.0 - sig))).astype(BF)
        db = (du * act).astype(BF)
        dao[i] = da
        dbo[i] = db
        dxe = (dotg(da, wg[i], NT) + dotg(db, wu[i], NT)).astype(BF)
        dg = RES * dsum
        hi = dg.astype(BF).astype(F32)
        low = dg - hi
        ln = lane((SLOTS, 128))
        ext = (
            jnp.where(ln == start + i, hi, 0.0) + jnp.where(ln == start + i + 64, low, 0.0)
        ).astype(BF)
        for k in range(8):
            dx[k, at, :D] = dxe[k * MOST : (k + 1) * MOST]
            dx[k, at, D:] = ext[k * MOST : (k + 1) * MOST]
        return carry

    lax.fori_loop(0, LOCAL, expert, 0)
    stores = []
    for k in range(8):
        hbuf[k] = dotg(pds[k], dx[k], TN).astype(BF)
        stores.append(pltpu.make_async_copy(hbuf.at[k], dhs[k], osem.at[0, k]))
        stores[-1].start()
    for k in range(8):
        gbuf[k, :, :D] = dotg(pds[k], rg[k], TN).astype(BF)
        stores.append(
            pltpu.make_async_copy(gbuf.at[k, :, pl.ds(0, D)], yall.at[order[k]], osem.at[1, k])
        )
        stores[-1].start()
    for c in stores:
        c.wait()


def experts(order, first, h2s, xs, wr, pieces):
    return pl.pallas_call(
        experts_kernel,
        out_shape=(
            sds((LOCAL, SLOTS, D), BF),
            sds((LOCAL, SLOTS, D), BF),
            sds((LOCAL, SLOTS, FF), BF),
            sds((LOCAL, SLOTS, FF), BF),
            sds((LOCAL, SLOTS, FF), BF),
        )
        + tuple(sds((TOK, D + 128), BF) for _ in range(8))
        + (sds((8, TOK, D), BF),),
        in_specs=[SM] * 2 + [HB] * 16 + specs(1) + [HB] * 2,
        out_specs=tuple(specs(5) + [HB] * 9),
        scratch_shapes=[
            pltpu.VMEM((LOCAL, D, FF), BF),
            pltpu.VMEM((LOCAL, D, FF), BF),
            pltpu.VMEM((LOCAL, 3, FF, FF), BF),
            pltpu.VMEM((8, TOK, D + 128), BF),
            pltpu.VMEM((8, TOK, D + 128), BF),
            pltpu.VMEM((8, ROWS, D), BF),
            pltpu.VMEM((8, ROWS, D + 128), BF),
            pltpu.VMEM((8, ROWS, TOK), BF),
            pltpu.VMEM((LOCAL, SLOTS, 128), F32),
            pltpu.SemaphoreType.DMA((3, 16)),
            pltpu.SemaphoreType.DMA((2, 8)),
            pltpu.SemaphoreType.DMA((2, 8)),
        ],
        compiler_params=params(60),
        cost_estimate=cost(24e9, 60e6),
        name="experts",
    )(order, first, *h2s, *xs, wr, pieces, pieces.reshape(16, 15, 3, 32, FF))


def expert_grads_kernel(fidx, x, dr, u, da, db, *refs):
    outs, scr, scr2 = refs[:2], refs[2], refs[3]
    xt = x[0]
    for m, d in ((0, da), (1, db)):
        scr[...] = dotg(xt, d[0], TN).astype(BF)
        for k in range(16):
            outs[k // 8][k % 8, m, 0] = scr[pl.ds(pl.multiple_of(fidx[k] * 96, 32), 96), :]
    scr2[...] = dotg(u[0], dr[0], TN).astype(BF)
    for k in range(16):
        at = pl.ds(pl.multiple_of(fidx[k] * 32, 32), 32)
        for j in range(3):
            outs[k // 8][k % 8, 2, 0, j * 32 : (j + 1) * 32, :] = scr2[at, j * FF : (j + 1) * FF]


def expert_grads(fidx, x, dr, u, da, db):
    row = lambda i: (i, 0, 0)
    return pl.pallas_call(
        expert_grads_kernel,
        grid=(LOCAL,),
        out_shape=tuple(sds((8, 3, LOCAL, 96, FF), BF) for _ in range(2)),
        in_specs=[
            SM,
            pl.BlockSpec((1, SLOTS, D), row),
            pl.BlockSpec((1, SLOTS, D), row),
            pl.BlockSpec((1, SLOTS, FF), row),
            pl.BlockSpec((1, SLOTS, FF), row),
            pl.BlockSpec((1, SLOTS, FF), row),
        ],
        out_specs=tuple(
            pl.BlockSpec((8, 3, 1, 96, FF), lambda i: (0, 0, i, 0, 0)) for _ in range(2)
        ),
        scratch_shapes=[pltpu.VMEM((D, FF), BF), pltpu.VMEM((FF, D), BF)],
        compiler_params=params(),
        cost_estimate=cost(8e9, 40e6),
        name="expert_grads",
    )(fidx, x, dr, u, da, db)


def home_kernel(*refs):
    parts = refs[:5]
    x2, h2, gain, g, routes, wr, w_out = refs[5:12]
    dx2o, dod, grouter, gmid = refs[12:]
    total = parts[0][...].astype(F32)
    for p in parts[1:]:
        total = total + p[...].astype(F32)
    ext = total[:, D:]
    ln = lane((TOK, 128))
    dg = jnp.where(ln < EXPERTS, ext + pltpu.roll(ext, 64, 1), 0.0)
    member = ln == routes[:, 0:1]
    for j in range(1, TOP):
        member = member | (ln == routes[:, j : j + 1])
    logits = jnp.where(member, dot(h2[...], wr[...]), -1e30)
    e = jnp.where(member, jnp.exp(logits - jnp.max(logits, axis=1, keepdims=True)), 0.0)
    gates = e / jnp.sum(e, axis=1, keepdims=True)
    dl = gates * (dg - jnp.sum(gates * dg, axis=1, keepdims=True))
    hi = dl.astype(BF)
    low = (dl - hi.astype(F32)).astype(BF)
    dh = total[:, :D] + dotg(hi, wr[...], NT) + dotg(low, wr[...], NT)
    grouter[...] = dotg(h2[...], hi, TN) + dotg(h2[...], low, TN)
    v = x2[...]
    scaler = lax.rsqrt(jnp.mean(v * v, axis=-1, keepdims=True) + EPSILON)
    n = v * scaler
    gmid[...] = jnp.sum(dh * n, axis=0, keepdims=True)
    inner = dh * gain[...]
    dx2 = g[...].astype(F32) + scaler * (inner - n * jnp.mean(inner * n, axis=-1, keepdims=True))
    dx2o[...] = dx2
    dao = dx2.astype(BF)
    pad = jnp.zeros((TOK, 256 - QW), BF)
    for s in range(8):
        do = (RES * dotg(dao, w_out[s * QW : (s + 1) * QW, :], NT)).astype(BF)
        dod[s] = jnp.concatenate([do, pad, dao[:, s * QW : (s + 1) * QW], pad], axis=1)


def home(parts, x2, h2, gain, g, routes, wr, w_out):
    return pl.pallas_call(
        home_kernel,
        grid=(1,),
        out_shape=(
            sds((TOK, D), F32),
            sds((8, TOK, 512), BF),
            sds((D, 128), F32),
            sds((1, D), F32),
        ),
        in_specs=specs(11) + [OUT_BLOCK],
        out_specs=tuple(specs(4)),
        compiler_params=params(),
        cost_estimate=cost(3e9, 10e6),
        name="home_bwd",
    )(*parts, x2, h2, gain, g, routes, wr, w_out)


def attn_bwd_kernel(order, *refs):
    xs = refs[:8]
    qkv, lse, dod, w, cosb, sinb, posq, posk = refs[8:16]
    dhs = refs[16:24]
    dqkv, gpre, kk, vv, dkt, dvt = refs[24:]
    lo = lane((TOK, 128)) < 64
    for b in range(8):
        rows = slice(b * TOK, (b + 1) * TOK)
        t1 = qkv[rows, 128:256].astype(F32)
        t2 = qkv[rows, 256:].astype(F32)
        kk[rows, :] = jnp.where(lo, pltpu.roll(t1, 64, 1), t1).astype(BF)
        vv[rows, :] = (t2 + pltpu.roll(t2, 64, 1)).astype(BF)
    dkt[...] = jnp.zeros_like(dkt)
    dvt[...] = jnp.zeros_like(dvt)

    def block(b, carry):
        rows = pl.ds(pl.multiple_of(b * TOK, TOK), TOK)
        vis = posk[...] <= posq[rows, :]
        t0 = qkv[rows, :128]
        t1 = qkv[rows, 128:256]
        d0 = dod[b, :, :128]
        d1 = dod[b, :, 128:256]
        zero = jnp.zeros_like(t0)
        sides = (
            (jnp.where(lo, t0, zero), jnp.where(lo, d0, zero)),
            (jnp.where(lo, zero, t0), jnp.where(lo, zero, d0)),
            (jnp.where(lo, t1, zero), jnp.where(lo, d1, zero)),
        )
        dqs = []
        dkacc = jnp.zeros((128, SEQ_LEN), F32)
        dvacc = jnp.zeros((128, SEQ_LEN), F32)
        for h, (q, do) in enumerate(sides):
            s = dotg(q, kk[...], NT) * SCORE_SCALE
            p = jnp.where(vis, jnp.exp(s - lse[rows, h : h + 1]), 0.0)
            dp = dotg(do, vv[...], NT)
            delta = jnp.sum(p * dp, axis=-1, keepdims=True)
            ds = (p * (dp - delta)).astype(BF)
            pb = p.astype(BF)
            dqs.append(dot(ds, kk[...]))
            dkacc = dkacc + dotg(q, ds, TN)
            dvacc = dvacc + dotg(do, pb, TN)
        dkt[...] += dkacc
        dvt[...] += dvacc
        dq0 = jnp.where(lo, dqs[0], dqs[1]) * SCORE_SCALE
        dq1 = dqs[2] * SCORE_SCALE
        cos = cosb[rows, :]
        sin = sinb[rows, :]
        dqkv[rows, :128] = (dq0 * cos - swap32(dq0) * sin).astype(BF)
        dqkv[rows, 128:256] = jnp.where(lo, dq1 * cos - swap32(dq1) * sin, 0.0).astype(BF)
        return carry

    lax.fori_loop(0, 8, block, 0)
    dk = jnp.transpose(dkt[...]) * SCORE_SCALE
    dv = jnp.transpose(dvt[...])
    low = lane((SEQ_LEN, 128)) < 64
    dk = dk + pltpu.roll(dk, 64, 1)
    dv = dv + pltpu.roll(dv, 64, 1)
    dk = dk * cosb[...] - swap32(dk) * sinb[...]
    dqkv[:, 128:256] = jnp.where(low, dqkv[:, 128:256].astype(F32), dk).astype(BF)
    dqkv[:, 256:] = jnp.where(low, dv, 0.0).astype(BF)
    acc = jnp.zeros((1, D), F32)
    for k in range(8):
        rows = pl.ds(pl.multiple_of(order[k] * TOK, TOK), TOK)
        dh = dotg(dqkv[rows, :], w[...], NT)
        dhs[k][...] = dh.astype(BF)
        x = xs[k][...].astype(F32)
        scaler = lax.rsqrt(jnp.mean(x * x, axis=-1, keepdims=True) + EPSILON)
        acc = acc + jnp.sum(dh * (x * scaler), axis=0, keepdims=True)
    gpre[...] = acc


def attn_bwd(order, xs, qkv, lse, dod, w, cosb, sinb, posq, posk):
    return pl.pallas_call(
        attn_bwd_kernel,
        grid=(1,),
        out_shape=tuple(sds((TOK, D), BF) for _ in range(8))
        + (sds((SEQ_LEN, 384), BF), sds((1, D), F32)),
        in_specs=[SM] + [X_BLOCK] * 8 + specs(3) + [QKV_BLOCK] + specs(4),
        out_specs=tuple(specs(10)),
        scratch_shapes=[
            pltpu.VMEM((SEQ_LEN, 128), BF),
            pltpu.VMEM((SEQ_LEN, 128), BF),
            pltpu.VMEM((128, SEQ_LEN), F32),
            pltpu.VMEM((128, SEQ_LEN), F32),
        ],
        compiler_params=params(),
        cost_estimate=cost(12e9, 14e6),
        name="attn_bwd",
    )(order, *xs, qkv, lse, dod, w, cosb, sinb, posq, posk)


def attn_grads_kernel(h1, dqkv, dod, ocs, grouter, gpre, gmid, outs, scr):
    scr[:, :384] = dotg(h1[...], dqkv[...], TN).astype(BF)
    acc = jnp.zeros((D, 256), F32)
    for k in range(8):
        acc = acc + dotg(ocs[k], dod[k, :, 256:], TN)
    scr[:, 384:] = (RES * acc).astype(BF)
    pre = jnp.transpose(jnp.broadcast_to(gpre[...], (128, D)))
    mid = jnp.transpose(jnp.broadcast_to(gmid[...], (128, D)))
    ln = lane((D, 128))
    ext = pltpu.roll(grouter[...], 64, 1)
    ext = jnp.where(ln == 104, pre, jnp.where(ln == 105, mid, ext)).astype(BF)
    scr[:, 256:384] = jnp.where(ln < 64, scr[:, 256:384], ext)
    for k in range(16):
        outs[k] = scr[k * 96 : (k + 1) * 96, :]


def attn_grads(h1, dqkv, dod, ocs, grouter, gpre, gmid):
    return pl.pallas_call(
        attn_grads_kernel,
        out_shape=sds((16, 96, 640), BF),
        in_specs=specs(7),
        out_specs=specs(1)[0],
        scratch_shapes=[pltpu.VMEM((D, 640), BF)],
        compiler_params=params(),
        cost_estimate=cost(4e9, 12e6),
        name="attn_grads",
    )(h1, dqkv, dod, ocs, grouter, gpre, gmid)


def expert_out_kernel(keep, got, a, b, c, gate, up, down):
    for m, out in ((0, gate), (1, up), (2, down)):
        for e in range(LOCAL):
            i = m * LOCAL + e
            v = keep[0, m, e].astype(F32) + got[0, m, e].astype(F32)
            v = v + a[i].astype(F32) + b[i].astype(F32) + c[i].astype(F32)
            if m < 2:
                out[e] = v
            else:
                for j in range(3):
                    out[e, :, j * FF : (j + 1) * FF] = v[j * 32 : (j + 1) * 32]


def expert_out(keep, got, parts):
    mine = pl.BlockSpec((1, 3, LOCAL, 96, FF), lambda i: (0, 0, 0, 0, 0))
    return pl.pallas_call(
        expert_out_kernel,
        grid=(1,),
        out_shape=(
            sds((LOCAL, 96, FF), F32),
            sds((LOCAL, 96, FF), F32),
            sds((LOCAL, 32, D), F32),
        ),
        in_specs=[mine, mine] + specs(3),
        out_specs=tuple(specs(3)),
        compiler_params=params(),
        cost_estimate=cost(1e6, 10e6),
        name="expert_out",
    )(keep, got, *parts)


def attn_out_kernel(full, gq, gk, gv, go, ext):
    pick = lambda lo, hi: jnp.concatenate([full[c, :, lo:hi] for c in range(8)], axis=1)
    gq[...] = pick(0, QW).astype(F32)
    gk[...] = pick(QW, QW + 64).astype(F32)
    gv[...] = pick(QW + 64, QW + 128).astype(F32)
    go[...] = pick(384, 384 + QW).astype(F32)
    total = full[0, :, 256:384].astype(F32)
    for c in range(1, 8):
        total = total + full[c, :, 256:384].astype(F32)
    ext[...] = pltpu.roll(total, 64, 1)


def attn_out(full):
    return pl.pallas_call(
        attn_out_kernel,
        out_shape=(
            sds((96, D), F32),
            sds((96, 512), F32),
            sds((96, 512), F32),
            sds((96, D), F32),
            sds((96, 128), F32),
        ),
        in_specs=specs(1),
        out_specs=tuple(specs(5)),
        compiler_params=params(),
        cost_estimate=cost(1e6, 3e6),
        name="attn_out",
    )(full)


def input_grad_kernel(*refs):
    parts = refs[:5]
    x, dx2, gain, out = refs[5:]
    dh = parts[0][...].astype(F32)
    for p in parts[1:]:
        dh = dh + p[...].astype(F32)
    v = x[...].astype(F32)
    scaler = lax.rsqrt(jnp.mean(v * v, axis=-1, keepdims=True) + EPSILON)
    n = v * scaler
    inner = dh * gain[...]
    dx1 = scaler * (inner - n * jnp.mean(inner * n, axis=-1, keepdims=True))
    out[...] = (dx2[...] + dx1).astype(BF)


def input_grad(parts, x, dx2, gain):
    return pl.pallas_call(
        input_grad_kernel,
        out_shape=sds((TOK, D), BF),
        in_specs=specs(8),
        out_specs=specs(1)[0],
        compiler_params=params(),
        cost_estimate=cost(1e6, 4e6),
        name="input_grad",
    )(*parts, x, dx2, gain)


def on_device(
    inputs,
    block_order,
    routes,
    pre_gain,
    w_query,
    w_key,
    w_value,
    w_out,
    w_router,
    mid_gain,
    w_gate,
    w_up,
    w_down,
    cotangent,
):
    ci = lax.axis_index("ctx")
    fi = lax.axis_index("fsdp")
    kr = jnp.arange(8, dtype=jnp.int32)
    order = ((ci // 4) ^ (kr // 4)) * 4 + (ci % 4 + kr % 4) % 4
    chips = ((fi // 4 + kr % 4) % 4) * 4 + (((fi // 2) % 2) ^ (kr // 4)) * 2
    fidx = jnp.concatenate([chips + fi % 2, chips + (1 - fi % 2)]).astype(jnp.int32)
    first = (ci * LOCAL).reshape(1).astype(jnp.int32)
    order = order.astype(jnp.int32)

    x = inputs[0]
    g = cotangent[0]
    xg = jnp.concatenate([x, g, routes[0].astype(BF), jnp.zeros((TOK, 120), BF)], axis=1)
    xs = gather2(xg, cs)

    q_c = lax.dynamic_slice_in_dim(w_query, ci * QW, QW, 1)
    k_c = lax.dynamic_slice_in_dim(w_key, ci * 64, 64, 1)
    v_c = lax.dynamic_slice_in_dim(w_value, ci * 64, 64, 1)
    pack = jnp.concatenate(
        [w_out, q_c, k_c, v_c, w_router, pre_gain[:, None], mid_gain[:, None], jnp.zeros((96, 22), BF)],
        axis=1,
    )
    weights = lax.all_gather(pack, "fsdp", axis=0, tiled=True)
    weights = after(weights, *xs)
    pre_row = weights[:, 1896:1897].reshape(1, D).astype(F32)
    mid_row = weights[:, 1897:1898].reshape(1, D).astype(F32)
    wr = weights[:, 1856:1896]
    wr_pad = jnp.pad(wr, ((0, 0), (0, 88)))
    wr_t = jnp.pad(jnp.roll(jnp.transpose(wr), -ci * LOCAL, axis=0), ((0, 8), (0, 0)))

    down3 = w_down.reshape(LOCAL, 32, 3, FF).transpose(0, 2, 1, 3).reshape(LOCAL, 96, FF)
    shard = jnp.concatenate([w_gate, w_up, down3], axis=0)
    pieces = lax.all_gather(shard, "fsdp", axis=0, tiled=False)

    span = SEQ_LEN // block_order.shape[0]
    pos = (block_order[:, None] * span + jnp.arange(span, dtype=jnp.int32)[None, :]).reshape(SEQ_LEN)
    freqs = THETA_BASE ** (-2.0 * jnp.arange(32, dtype=F32) / HEAD_DIM)
    angles = pos.astype(F32)[:, None] * freqs[None, :]
    cos = jnp.cos(angles)
    sin = jnp.sin(angles)
    cosb = jnp.concatenate([cos, cos, cos, cos], axis=1)
    sinb = jnp.concatenate([-sin, sin, -sin, sin], axis=1)
    posq = pos[:, None]
    posk = pos[None, :]

    h1, qkv, o, lse = attn_fwd(order, xs, weights, pre_row, cosb, sinb, posq, posk)
    oa = lax.all_to_all(o, "ctx", 0, 0, tiled=True)
    x2, h2, oc = out_proj(oa, weights, x, mid_row)
    h2s = gather2(h2, cs)
    ocb = jnp.broadcast_to(after(oc, *h2s), (8, TOK, D))
    ocs = lax.all_to_all(ocb, "ctx", 0, 0, tiled=True)
    outs = experts(order, first, h2s, xs, wr_t, pieces)
    xe, dre, ue, dae, dbe = outs[:5]
    dhs, yall = list(outs[5:13]), outs[13]
    parts = scatter2_parts(dhs, cs)
    keep, give = expert_grads(fidx, after(xe, ocs), dre, ue, dae, dbe)
    got = fs(give, 0, 0, 1)

    def chips(*done):
        kept, swapped = lax.optimization_barrier((keep, got) + done)[:2]
        kept = kept.reshape(8, 15, 96, FF)
        swapped = swapped.reshape(8, 15, 96, FF)
        return lambda k: (kept[k], swapped[k])

    e1 = scatter3_first(add_low(*chips()(6)), fs)
    dx2, dod, grouter, gmid = home(
        parts, x2, h2, after(mid_row, got), g, routes[0], wr_pad, weights
    )
    dod = lax.all_to_all(dod, "ctx", 0, 0, tiled=True)
    chip = chips(*e1)
    e2 = scatter3_second(chip(2), chip(5), chip(7), e1)
    dod = after(dod, *e2)
    chip = chips(*e2)
    e2 = scatter3_send(e2, fs)
    yg = lax.all_to_all(after(yall, dod), "ctx", 0, 0, tiled=True)
    ab = attn_bwd(order, xs, qkv, lse, dod, weights, cosb, sinb, posq, posk)
    dh1s, dqkv, gpre = ab[:8], ab[8], ab[9]
    p1 = scatter2_parts(dh1s, cs)
    e3 = scatter3_third(chip(1), chip(3), chip(4), e2)
    ag = attn_grads(h1, dqkv, dod, ocs, grouter, gpre, after(gmid, *e3))
    e3 = (fs(e3[0], 1), fs(e3[1], -1), fs(e3[2], 0, 1))
    ag = lax.all_to_all(after(ag, yg), "fsdp", 0, 0, tiled=True)
    ag = after(ag, *p1[1:], *e3)
    ashard = jnp.sum(ag.astype(F32), axis=0).astype(BF)
    ashard = jnp.broadcast_to(ashard, (8, 96, 640))
    full = lax.all_to_all(ashard, "ctx", 0, 0, tiled=True)
    gq, gk, gv, go, ext = attn_out(full)
    gate, up, down = expert_out(keep, got, e3)

    output = (x2 + RES * jnp.sum(yg.astype(F32), axis=0)).astype(BF)[None]
    grad_input = input_grad(p1, x, dx2, pre_row)[None]
    return (
        output,
        grad_input,
        ext[:, 40],
        gq,
        gk,
        gv,
        go,
        ext[:, :40],
        ext[:, 41],
        gate,
        up,
        down,
    )


def solution(mesh):
    return jax.shard_map(
        on_device,
        mesh=mesh,
        in_specs=(
            P("fsdp", "ctx", None),
            P(),
            P("fsdp", "ctx", None),
            P("fsdp"),
            P("fsdp", None),
            P("fsdp", None),
            P("fsdp", None),
            P("fsdp", None),
            P("fsdp", None),
            P("fsdp"),
            P("ctx", "fsdp", None),
            P("ctx", "fsdp", None),
            P("ctx", "fsdp", None),
            P("fsdp", "ctx", None),
        ),
        out_specs=(
            P("fsdp", "ctx", None),
            P("fsdp", "ctx", None),
            P("fsdp"),
            P("fsdp", None),
            P("fsdp", None),
            P("fsdp", None),
            P("fsdp", None),
            P("fsdp", None),
            P("fsdp"),
            P("ctx", "fsdp", None),
            P("ctx", "fsdp", None),
            P("ctx", "fsdp", None),
        ),
        check_vma=False,
    )
```

time: 1480 us -> 559 us (0.38)
  waiting for transfers between devices: 973 us -> 177 us
  blocking collectives: 156 us -> 0 us
  matrix products: 128 us -> 0 us
  Pallas kernels: 0 us -> 126 us
  starting transfers between devices: 27.6 us -> 148 us
  local copies, waits for them, and re-layouts: 97.4 us -> 43.2 us
  other arithmetic: 70.4 us -> 39.1 us
    reduce_scatter x7 -> x0, waiting for transfers between devices: 523 us -> none  [the longest x1 93.6 us: on_device(): lax.psum_scatter(grad_gate_full.astype(jnp.bfloat16), 'fsdp', scatter_dim...]
    all_gather x9 -> x2, waiting for transfers between devices: 213 us -> 10.3 us  [the longest x1 10.3 us: on_device(): pieces = lax.all_gather(shard, 'fsdp', axis=0, tiled=False)]
    ppermute x0 -> x41, waiting for transfers between devices: none -> 149 us  [the longest x28 141 us: cs(): return lax.ppermute(v, 'ctx', ctx_pairs(dr, dp))]
    dot_general x32 -> x0, matrix products: 128 us -> none  [the longest x1 9.84 us: on_device(): jnp.einsum('end,efd->enf', grad_recv, down_full, preferred_element_type=j...]
    pallas_call x0 -> x10, Pallas kernels: none -> 126 us  [the longest x1 35.4 us: experts(): pl.pallas_call(experts_kernel, out_shape=(sds((LOCAL, SLOTS, D), BF), sds...]
    unnamed x21 -> x2, waiting for transfers between devices: 110 us -> 0.03 us
    ppermute x0 -> x41, starting transfers between devices: none -> 110 us  [the longest x28 77.8 us: cs(): return lax.ppermute(v, 'ctx', ctx_pairs(dr, dp))]
    all_to_all x3 -> x6, waiting for transfers between devices: 102 us -> 17.5 us  [the longest x1 11.1 us: on_device(): oa = lax.all_to_all(o, 'ctx', 0, 0, tiled=True)]
  transfers between devices with their start and end apart: 22 -> 49, of which waited for: 21 -> 21; matrix products, arithmetic and copies ran while one was open for 14% -> 11% of each run, Pallas kernels for 0% -> 19%
where the time goes in v1:
time: 559 us; the launch traced here: 548 us
  waiting for transfers between devices  177 us (32%)
  starting transfers between devices  148 us (26%)
  Pallas kernels  126 us (23%)
  local copies, waits for them, and re-layouts  43.2 us (8%)
  other arithmetic  39.1 us (7%)
  between operations  15.1 us (3%)
    ppermute x28, waiting for transfers between devices, cs(): return lax.ppermute(v, 'ctx', ctx_pairs(dr, dp))  141 us
    ppermute x28, starting transfers between devices, cs(): return lax.ppermute(v, 'ctx', ctx_pairs(dr, dp))  77.8 us
    pallas_call x1, Pallas kernels, experts(): pl.pallas_call(experts_kernel, out_shape=(sds((LOCAL, SLOTS, D), BF), sds...  35.4 us
    ppermute x13, starting transfers between devices, fs(): return lax.ppermute(v, 'fsdp', fsdp_pairs(dr, dp, dc))  32.1 us
    pallas_call x1, Pallas kernels, attn_bwd(): pl.pallas_call(attn_bwd_kernel, grid=(1,), out_shape=tuple((sds((TOK, D),...  23.3 us
    convert_element_type x12, other arithmetic, add_low(): return total.astype(BF)  19.3 us
    pallas_call x1, Pallas kernels, attn_fwd(): pl.pallas_call(attn_fwd_kernel, grid=(1,), out_shape=(sds((SEQ_LEN, D), B...  18.6 us
    pallas_call x1, Pallas kernels, expert_grads(): pl.pallas_call(expert_grads_kernel, grid=(LOCAL,), out_shape=tuple((sds((...  17 us
  transfers between devices with their start and end apart: 49, of which 21 were waited for; matrix products, arithmetic and copies ran while one was open for 11% of the time, Pallas kernels for 19%

profile of v1, /device:TPU:17, one launch (start us, length us, event | category | flops | bytes accessed | tf_op | source)
XLA Modules:
  0.0 548.3 jit_solution(1738193515201361924)
XLA Ops:
  24.8 13.1 %collective-permute-done.3.refs_4_.refs_12_ = bf16[128,3200]{1,0:T(8,128)(2,1)S(1)} collective-permute-done((bf16[128,3200]{1,0:T(8,128)(2,1)S(1)}, bf16[128,3200]{1,0:T(8,128)(2,1)S(1)}, u32[]{:S(2)}, u32[]{:S(2)}) %collective-permute-start.3) | collective-permute-done | bytes 819232 | tf_op jit(solution)/shard_map/ppermute | solution.py:58
  49.2 9.5 %collective-permute-done.1.refs_2_.refs_10_ = bf16[128,3200]{1,0:T(8,128)(2,1)} collective-permute-done((bf16[128,3200]{1,0:T(8,128)(2,1)S(1)}, bf16[128,3200]{1,0:T(8,128)(2,1)}, u32[]{:S(2)}, u32[]{:S(2)}) %collective-permute-start.1) | collective-permute-done | bytes 819232 | tf_op jit(solution)/shard_map/ppermute | solution.py:58
  59.6 16.2 %collective-permute-done.6.refs_7_.refs_15_ = bf16[128,3200]{1,0:T(8,128)(2,1)} collective-permute-done((bf16[128,3200]{1,0:T(8,128)(2,1)S(1)}, bf16[128,3200]{1,0:T(8,128)(2,1)}, u32[]{:S(2)}, u32[]{:S(2)}) %collective-permute-start.6) | collective-permute-done | bytes 819232 | tf_op jit(solution)/shard_map/ppermute | solution.py:58
  75.8 18.0 %collective-permute-done.5.refs_6_.refs_14_ = bf16[128,3200]{1,0:T(8,128)(2,1)} collective-permute-done((bf16[128,3200]{1,0:T(8,128)(2,1)S(1)}, bf16[128,3200]{1,0:T(8,128)(2,1)}, u32[]{:S(2)}, u32[]{:S(2)}) %collective-permute-start.5) | collective-permute-done | bytes 819232 | tf_op jit(solution)/shard_map/ppermute | solution.py:58
  96.1 18.6 %attn_fwd.1 = (bf16[1024,1536]{1,0:T(8,128)(2,1)}, bf16[1024,384]{1,0:T(8,128)(2,1)}, bf16[8,128,256]{2,1,0:T(8,128)(2,1)}, f32[1024,128]{1,0:T(8,128)}) custom-call(s32[8]{0:T(128)} %fusion.8.order, bf16[128,3200]{1,0:T(8,128)(2,1)} %copy-done.17, bf16[128,3200]{1,0:T(8,128)(2,1)} %collective-permute-done.refs_1_.refs_9_, ...), custom_call_target="tpu_custom_call" | custom-call | flops 6000000000 | bytes 12000000 | tf_op jit(solution)/shard_map/attn_fwd/pallas_call | solution.py:240
  120.2 11.1 %all-to-all-done.oa = bf16[8,128,256]{2,1,0:T(8,128)(2,1)S(1)} async-done(((bf16[8,128,256]{2,1,0:T(8,128)(2,1)}), bf16[8,128,256]{2,1,0:T(8,128)(2,1)S(1)}, u32[]{:S(2)}, u32[]{:S(2)}) %all-to-all-start) | async-done | bytes 524320 | tf_op jit(solution)/shard_map/all_to_all | solution.py:794
  139.9 8.3 %collective-permute-done.10.refs_4_ = bf16[128,1536]{1,0:T(8,128)(2,1)S(1)} collective-permute-done((bf16[128,1536]{1,0:T(8,128)(2,1)}, bf16[128,1536]{1,0:T(8,128)(2,1)S(1)}, u32[]{:S(2)}, u32[]{:S(2)}) %collective-permute-start.10) | collective-permute-done | bytes 393248 | tf_op jit(solution)/shard_map/ppermute | solution.py:58
  158.7 14.6 %collective-permute-done.13.refs_7_ = bf16[128,1536]{1,0:T(8,128)(2,1)S(1)} collective-permute-done((bf16[128,1536]{1,0:T(8,128)(2,1)S(1)}, bf16[128,1536]{1,0:T(8,128)(2,1)S(1)}, u32[]{:S(2)}, u32[]{:S(2)}) %collective-permute-start.13) | collective-permute-done | bytes 393248 | tf_op jit(solution)/shard_map/ppermute | solution.py:58
  188.8 10.3 %all-gather.6.cloned.1.call-done = bf16[240,96,512]{2,1,0:T(8,128)(2,1)} async-done(((bf16[15,96,512]{2,1,0:T(8,128)(2,1)}), bf16[240,96,512]{2,1,0:T(8,128)(2,1)}) %all-gather.6.cloned.1.call-update) | async-done | bytes 23592976 | tf_op jit(solution)/shard_map/all_gather | solution.py:780
  199.1 35.4 %experts.1 = (bf16[5,256,1536]{2,1,0:T(8,128)(2,1)}, bf16[5,256,1536]{2,1,0:T(8,128)(2,1)}, bf16[5,256,512]{2,1,0:T(8,128)(2,1)}, bf16[5,256,512]{2,1,0:T(8,128)...) custom-call(s32[8]{0:T(128)} %fusion.8.order, ...), custom_call_target="tpu_custom_call" | custom-call | flops 24000000000 | bytes 60000000 | tf_op jit(solution)/shard_map/experts/pallas_call | solution.py:402
  234.6 17.0 %expert_grads.1 = (bf16[8,3,5,96,512]{4,3,2,1,0:T(8,128)(2,1)}, bf16[8,3,5,96,512]{4,3,2,1,0:T(8,128)(2,1)}) custom-call(s32[16]{0:T(128)} %pad_add_fusion.fidx, bf16[5,256,1536]{2,1,0:T(8,128)(2,1)} %get-tuple-element.88.x, bf16[5,256,1536]{2,1,0:T(8,128)(2,1)} %get-tuple-element.89.dr, bf16[5,256,512]{2,1,0:T(8,128)(2,1)} %get-tuple-element.90.u, ...), custom_call_target="tpu_custom_call" | custom-call | flops 8000000000 | bytes 40000000 | tf_op jit(solution)/shard_map/expert_grads/pallas_call | solution.py:451
  252.8 27.7 %collective-permute-start.18 = (bf16[128,1664]{1,0:T(8,128)(2,1)S(1)}, bf16[128,1664]{1,0:T(8,128)(2,1)S(1)}, u32[]{:S(2)}, u32[]{:S(2)}) collective-permute-start(bf16[128,1664]{1,0:T(8,128)(2,1)S(1)} %copy-done.37), channel_id=1, source_target_pairs={{0,32},{16,48},{32,0},{48,16},{64,96},{80,112},{96,64},{112,80},{1... | collective-permute-start | bytes 1277960 | tf_op jit(solution)/shard_map/ppermute | solution.py:58
  282.4 18.0 %collective-permute-start.15 = (bf16[128,1664]{1,0:T(8,128)(2,1)S(1)}, bf16[128,1664]{1,0:T(8,128)(2,1)S(1)}, u32[]{:S(2)}, u32[]{:S(2)}) collective-permute-start(bf16[128,1664]{1,0:T(8,128)(2,1)S(1)} %copy-done.31), channel_id=1, source_target_pairs={{0,32},{16,48},{32,0},{48,16},{64,96},{80,112},{96,64},{112,80},{1... | collective-permute-start | bytes 1277960 | tf_op jit(solution)/shard_map/ppermute | solution.py:58
  309.4 17.9 %collective-permute-start.23 = (bf16[5,96,512]{2,1,0:T(8,128)(2,1)S(1)}, bf16[5,96,512]{2,1,0:T(8,128)(2,1)S(1)}, u32[]{:S(2)}, u32[]{:S(2)}) collective-permute-start(bf16[5,96,512]{2,1,0:T(8,128)(2,1)S(1)} %get-tuple-element.212), channel_id=1, source_target_pairs={{0,4},{1,5},{2,6},{3,7},{4,8},{5,9},{6,10},{7,11},{8,12},{9,13},{1... | collective-permute-start | bytes 1474568 | tf_op jit(solution)/shard_map/ppermute | solution.py:62
  329.2 7.7 %home_bwd.1 = (f32[128,1536]{1,0:T(8,128)}, bf16[8,128,512]{2,1,0:T(8,128)(2,1)}, f32[1536,128]{1,0:T(8,128)}, f32[1,1536]{1,0:T(1,128)}) custom-call(bf16[128,1664]{1,0:T(8,128)(2,1)} %get-tuple-element.77.refs_0_, bf16[128,1664]{1,0:T(8,128)(2,1)} %copy-done.33, bf16[128,1664]{1,0:T(8,128)(2,1)} %copy-done.34, bf16[128,1664]{1,0:T(8,128)(2,1)} %copy-done.35, ...), custom_call_target="tpu_custom_call" | custom-call | flops 3000000000 | bytes 10000000 | tf_op jit(solution)/shard_map/home_bwd/pallas_call | solution.py:509
  351.7 7.8 %collective-permute-start.36 = (bf16[7,96,512]{2,1,0:T(8,128)(2,1)}, bf16[7,96,512]{2,1,0:T(8,128)(2,1)}, u32[]{:S(2)}, u32[]{:S(2)}) collective-permute-start(bf16[7,96,512]{2,1,0:T(8,128)(2,1)} %pad_maximum_fusion.6), channel_id=1, source_target_pairs={{0,4},{1,5},{2,6},{3,7},{4,8},{5,9},{6,10},{7,11},{8,12},{9,13},{1... | collective-permute-start | bytes 2064392 | tf_op jit(solution)/shard_map/ppermute | solution.py:62
  378.7 6.9 %all-to-all-start.3 = ((bf16[8,128,1536]{2,1,0:T(8,128)(2,1)}), bf16[8,128,1536]{2,1,0:T(8,128)(2,1)S(1)}, u32[]{:S(2)}, u32[]{:S(2)}) async-start(bf16[8,128,1536]{2,1,0:T(8,128)(2,1)} %get-tuple-element.102), calls=%async_computation.3 | async-start | bytes 6291456 | tf_op jit(solution)/shard_map/all_to_all | solution.py:822
  385.6 23.3 %attn_bwd.1 = (bf16[128,1536]{1,0:T(8,128)(2,1)}, bf16[128,1536]{1,0:T(8,128)(2,1)}, bf16[128,1536]{1,0:T(8,128)(2,1)}, bf16[128,1536]{1,0:T(8,128)(2,1)}, bf16[...) custom-call(s32[8]{0:T(128)} %fusion.8.order, ...), custom_call_target="tpu_custom_call" | custom-call | flops 12000000000 | bytes 14000000 | tf_op jit(solution)/shard_map/attn_bwd/pallas_call | solution.py:598
  417.7 7.6 %collective-permute-done.34 = bf16[8,96,512]{2,1,0:T(8,128)(2,1)S(1)} collective-permute-done((bf16[8,96,512]{2,1,0:T(8,128)(2,1)S(1)}, bf16[8,96,512]{2,1,0:T(8,128)(2,1)S(1)}, u32[]{:S(2)}, u32[]{:S(2)}) %collective-permute-start.34) | collective-permute-done | bytes 786464 | tf_op jit(solution)/shard_map/ppermute | solution.py:62
  428.2 8.6 %attn_grads.1 = bf16[16,96,640]{2,1,0:T(8,128)(2,1)} custom-call(bf16[1024,1536]{1,0:T(8,128)(2,1)} %get-tuple-element.114.h1, bf16[1024,384]{1,0:T(8,128)(2,1)} %get-tuple-element.115.dqkv, bf16[8,128,512]{2,1,0:T(8,128)(2,1)} %copy-done.16, bf16[8,128,1536]{2,1,0:T(8,128)(2,1)} %copy-done.11, f32[1536,128]{1,0:T(8,128)} %get-tuple-element.116.grouter, ...), custom_call_target="tpu_custom_call" | custom-call | flops 4000000000 | bytes 12000000 | tf_op jit(solution)/shard_map/attn_grads/pallas_call | solution.py:634
  436.8 9.8 %all-to-all-start.4 = ((bf16[16,96,640]{2,1,0:T(8,128)(2,1)}), bf16[16,96,640]{2,1,0:T(8,128)(2,1)}, u32[]{:S(2)}, u32[]{:S(2)}) async-start(bf16[16,96,640]{2,1,0:T(8,128)(2,1)} %attn_grads.1), calls=%async_computation.4 | async-start | bytes 3932160 | tf_op jit(solution)/shard_map/all_to_all | solution.py:829
  459.9 8.0 %collective-permute-done.29 = bf16[128,1536]{1,0:T(8,128)(2,1)S(1)} collective-permute-done((bf16[128,1536]{1,0:T(8,128)(2,1)}, bf16[128,1536]{1,0:T(8,128)(2,1)S(1)}, u32[]{:S(2)}, u32[]{:S(2)}) %collective-permute-start.29) | collective-permute-done | bytes 393248 | tf_op jit(solution)/shard_map/ppermute | solution.py:58
  473.8 13.6 %collective-permute-done.25.refs_1_ = bf16[128,1536]{1,0:T(8,128)(2,1)} collective-permute-done((bf16[128,1536]{1,0:T(8,128)(2,1)}, bf16[128,1536]{1,0:T(8,128)(2,1)}, u32[]{:S(2)}, u32[]{:S(2)}) %collective-permute-start.25) | collective-permute-done | bytes 393248 | tf_op jit(solution)/shard_map/ppermute | solution.py:58
  496.0 15.7 %collective-permute-done.31.refs_4_ = bf16[128,1536]{1,0:T(8,128)(2,1)} collective-permute-done((bf16[128,1536]{1,0:T(8,128)(2,1)S(1)}, bf16[128,1536]{1,0:T(8,128)(2,1)}, u32[]{:S(2)}, u32[]{:S(2)}) %collective-permute-start.31) | collective-permute-done | bytes 393248 | tf_op jit(solution)/shard_map/ppermute | solution.py:58
  (246 shorter events, 188.5 us)
Async XLA Ops:
  7.2 86.6 %all-gather.4.cloned.1.call-start = ((), (), s32[]{:S(2)}) async-start(), calls=%async_computation.6 | async-start | bytes 6266880 | tf_op jit(solution)/shard_map/all_gather | solution.py:770
  12.5 186.7 %all-gather.6.cloned.1.call-start = ((), (), s32[]{:S(2)}) async-start(), calls=%async_computation.7 | async-start | bytes 25067520 | tf_op jit(solution)/shard_map/all_gather | solution.py:780
  21.2 37.5 %collective-permute-start.1 = (bf16[128,3200]{1,0:T(8,128)(2,1)S(1)}, bf16[128,3200]{1,0:T(8,128)(2,1)}, u32[]{:S(2)}, u32[]{:S(2)}) collective-permute-start(bf16[128,3200]{1,0:T(8,128)(2,1)S(1)} %concatenate.44.refs_0_.refs_8_), channel_id=1, source_target_pairs={{0,32},{16,48},{32,0},{48,16},{64,96},{80,112},{96,64},{112,80},{1... | collective-permute-start | bytes 2457608 | tf_op jit(solution)/shard_map/ppermute | solution.py:58
  23.7 36.0 %collective-permute-start = (bf16[128,3200]{1,0:T(8,128)(2,1)S(1)}, bf16[128,3200]{1,0:T(8,128)(2,1)}, u32[]{:S(2)}, u32[]{:S(2)}) collective-permute-start(bf16[128,3200]{1,0:T(8,128)(2,1)S(1)} %concatenate.44.refs_0_.refs_8_), channel_id=1, source_target_pairs={{0,48},{16,0},{32,16},{48,32},{64,112},{80,64},{96,80},{112,96},{1... | collective-permute-start | bytes 2457608 | tf_op jit(solution)/shard_map/ppermute | solution.py:58
  38.0 37.8 %collective-permute-start.6 = (bf16[128,3200]{1,0:T(8,128)(2,1)S(1)}, bf16[128,3200]{1,0:T(8,128)(2,1)}, u32[]{:S(2)}, u32[]{:S(2)}) collective-permute-start(bf16[128,3200]{1,0:T(8,128)(2,1)S(1)} %collective-permute-done.3.refs_4_.refs_12_), channel_id=1, source_target_pairs={{0,16},{16,32},{32,48},{48,0},{64,80},{80,96},{96,112},{112,64},{1... | collective-permute-start | bytes 2457608 | tf_op jit(solution)/shard_map/ppermute | solution.py:58
  39.2 54.6 %collective-permute-start.5 = (bf16[128,3200]{1,0:T(8,128)(2,1)S(1)}, bf16[128,3200]{1,0:T(8,128)(2,1)}, u32[]{:S(2)}, u32[]{:S(2)}) collective-permute-start(bf16[128,3200]{1,0:T(8,128)(2,1)S(1)} %collective-permute-done.3.refs_4_.refs_12_), channel_id=1, source_target_pairs={{0,32},{16,48},{32,0},{48,16},{64,96},{80,112},{96,64},{112,80},{1... | collective-permute-start | bytes 2457608 | tf_op jit(solution)/shard_map/ppermute | solution.py:58
  41.8 52.1 %collective-permute-start.4 = (bf16[128,3200]{1,0:T(8,128)(2,1)S(1)}, bf16[128,3200]{1,0:T(8,128)(2,1)}, u32[]{:S(2)}, u32[]{:S(2)}) collective-permute-start(bf16[128,3200]{1,0:T(8,128)(2,1)S(1)} %collective-permute-done.3.refs_4_.refs_12_), channel_id=1, source_target_pairs={{0,48},{16,0},{32,16},{48,32},{64,112},{80,64},{96,80},{112,96},{1... | collective-permute-start | bytes 2457608 | tf_op jit(solution)/shard_map/ppermute | solution.py:58
  177.2 57.3 %all-to-all-start.1 = ((bf16[8,128,1536]{2,1,0:T(8,128)(2,1)}), bf16[8,128,1536]{2,1,0:T(8,128)(2,1)S(1)}, u32[]{:S(2)}, u32[]{:S(2)}) async-start(bf16[8,128,1536]{2,1,0:T(8,128)(2,1)} %broadcast_in_dim.32), calls=%async_computation.1 | async-start | bytes 6291456 | tf_op jit(solution)/shard_map/all_to_all | solution.py:798
  251.6 50.8 %collective-permute-start.21 = (bf16[8,3,5,96,512]{4,3,2,1,0:T(8,128)(2,1)}, bf16[8,3,5,96,512]{4,3,2,1,0:T(8,128)(2,1)S(1)}, u32[]{:S(2)}, u32[]{:S(2)}) collective-permute-start(bf16[8,3,5,96,512]{4,3,2,1,0:T(8,128)(2,1)} %get-tuple-element.93), channel_id=1, source_target_pairs={{0,1},{1,0},{2,3},{3,2},{4,5},{5,4},{6,7},{7,6},{8,9},{9,8},{10,11... | collective-permute-start | bytes 35389448 | tf_op jit(solution)/shard_map/ppermute | solution.py:62
  252.8 47.7 %collective-permute-start.18 = (bf16[128,1664]{1,0:T(8,128)(2,1)S(1)}, bf16[128,1664]{1,0:T(8,128)(2,1)S(1)}, u32[]{:S(2)}, u32[]{:S(2)}) collective-permute-start(bf16[128,1664]{1,0:T(8,128)(2,1)S(1)} %copy-done.37), channel_id=1, source_target_pairs={{0,32},{16,48},{32,0},{48,16},{64,96},{80,112},{96,64},{112,80},{1... | collective-permute-start | bytes 1277960 | tf_op jit(solution)/shard_map/ppermute | solution.py:58
  282.4 44.9 %collective-permute-start.15 = (bf16[128,1664]{1,0:T(8,128)(2,1)S(1)}, bf16[128,1664]{1,0:T(8,128)(2,1)S(1)}, u32[]{:S(2)}, u32[]{:S(2)}) collective-permute-start(bf16[128,1664]{1,0:T(8,128)(2,1)S(1)} %copy-done.31), channel_id=1, source_target_pairs={{0,32},{16,48},{32,0},{48,16},{64,96},{80,112},{96,64},{112,80},{1... | collective-permute-start | bytes 1277960 | tf_op jit(solution)/shard_map/ppermute | solution.py:58
  309.4 33.4 %collective-permute-start.24 = (bf16[5,96,512]{2,1,0:T(8,128)(2,1)}, bf16[5,96,512]{2,1,0:T(8,128)(2,1)S(1)}, u32[]{:S(2)}, u32[]{:S(2)}) collective-permute-start(bf16[5,96,512]{2,1,0:T(8,128)(2,1)} %get-tuple-element.211), channel_id=1, source_target_pairs={{0,12},{1,13},{2,14},{3,15},{4,0},{5,1},{6,2},{7,3},{8,4},{9,5},{1... | collective-permute-start | bytes 1474568 | tf_op jit(solution)/shard_map/ppermute | solution.py:62
  309.4 33.3 %collective-permute-start.23 = (bf16[5,96,512]{2,1,0:T(8,128)(2,1)S(1)}, bf16[5,96,512]{2,1,0:T(8,128)(2,1)S(1)}, u32[]{:S(2)}, u32[]{:S(2)}) collective-permute-start(bf16[5,96,512]{2,1,0:T(8,128)(2,1)S(1)} %get-tuple-element.212), channel_id=1, source_target_pairs={{0,4},{1,5},{2,6},{3,7},{4,8},{5,9},{6,10},{7,11},{8,12},{9,13},{1... | collective-permute-start | bytes 1474568 | tf_op jit(solution)/shard_map/ppermute | solution.py:62
  337.0 40.8 %all-to-all-start.2 = ((bf16[8,128,512]{2,1,0:T(8,128)(2,1)}), bf16[8,128,512]{2,1,0:T(8,128)(2,1)S(1)}, u32[]{:S(2)}, u32[]{:S(2)}) async-start(bf16[8,128,512]{2,1,0:T(8,128)(2,1)} %get-tuple-element.95), calls=%async_computation.2 | async-start | bytes 2097152 | tf_op jit(solution)/shard_map/all_to_all | solution.py:816
  351.7 57.2 %collective-permute-start.36 = (bf16[7,96,512]{2,1,0:T(8,128)(2,1)}, bf16[7,96,512]{2,1,0:T(8,128)(2,1)}, u32[]{:S(2)}, u32[]{:S(2)}) collective-permute-start(bf16[7,96,512]{2,1,0:T(8,128)(2,1)} %pad_maximum_fusion.6), channel_id=1, source_target_pairs={{0,4},{1,5},{2,6},{3,7},{4,8},{5,9},{6,10},{7,11},{8,12},{9,13},{1... | collective-permute-start | bytes 2064392 | tf_op jit(solution)/shard_map/ppermute | solution.py:62
  359.5 55.4 %collective-permute-start.33 = (bf16[8,96,512]{2,1,0:T(8,128)(2,1)}, bf16[8,96,512]{2,1,0:T(8,128)(2,1)}, u32[]{:S(2)}, u32[]{:S(2)}) collective-permute-start(bf16[8,96,512]{2,1,0:T(8,128)(2,1)} %pad_maximum_fusion.5), channel_id=1, source_target_pairs={{0,2},{1,3},{2,0},{3,1},{4,6},{5,7},{6,4},{7,5},{8,10},{9,11},{10,... | collective-permute-start | bytes 2359304 | tf_op jit(solution)/shard_map/ppermute | solution.py:62
  363.4 45.6 %collective-permute-start.37 = (bf16[7,96,512]{2,1,0:T(8,128)(2,1)}, bf16[7,96,512]{2,1,0:T(8,128)(2,1)}, u32[]{:S(2)}, u32[]{:S(2)}) collective-permute-start(bf16[7,96,512]{2,1,0:T(8,128)(2,1)} %slice.262), channel_id=1, source_target_pairs={{0,12},{1,13},{2,14},{3,15},{4,0},{5,1},{6,2},{7,3},{8,4},{9,5},{1... | collective-permute-start | bytes 2064392 | tf_op jit(solution)/shard_map/ppermute | solution.py:62
  363.4 49.2 %collective-permute-start.32 = (bf16[7,96,512]{2,1,0:T(8,128)(2,1)}, bf16[7,96,512]{2,1,0:T(8,128)(2,1)}, u32[]{:S(2)}, u32[]{:S(2)}) collective-permute-start(bf16[7,96,512]{2,1,0:T(8,128)(2,1)} %pad_maximum_fusion.7), channel_id=1, source_target_pairs={{0,4},{1,5},{2,6},{3,7},{4,8},{5,9},{6,10},{7,11},{8,12},{9,13},{1... | collective-permute-start | bytes 2064392 | tf_op jit(solution)/shard_map/ppermute | solution.py:62
  364.9 52.8 %collective-permute-start.35 = (bf16[8,96,512]{2,1,0:T(8,128)(2,1)}, bf16[8,96,512]{2,1,0:T(8,128)(2,1)}, u32[]{:S(2)}, u32[]{:S(2)}) collective-permute-start(bf16[8,96,512]{2,1,0:T(8,128)(2,1)} %pad_maximum_fusion.4), channel_id=1, source_target_pairs={{0,2},{1,3},{2,0},{3,1},{4,6},{5,7},{6,4},{7,5},{8,10},{9,11},{10,... | collective-permute-start | bytes 2359304 | tf_op jit(solution)/shard_map/ppermute | solution.py:62
  378.7 58.1 %all-to-all-start.3 = ((bf16[8,128,1536]{2,1,0:T(8,128)(2,1)}), bf16[8,128,1536]{2,1,0:T(8,128)(2,1)S(1)}, u32[]{:S(2)}, u32[]{:S(2)}) async-start(bf16[8,128,1536]{2,1,0:T(8,128)(2,1)} %get-tuple-element.102), calls=%async_computation.3 | async-start | bytes 6291456 | tf_op jit(solution)/shard_map/all_to_all | solution.py:822
  436.8 74.9 %all-to-all-start.4 = ((bf16[16,96,640]{2,1,0:T(8,128)(2,1)}), bf16[16,96,640]{2,1,0:T(8,128)(2,1)}, u32[]{:S(2)}, u32[]{:S(2)}) async-start(bf16[16,96,640]{2,1,0:T(8,128)(2,1)} %attn_grads.1), calls=%async_computation.4 | async-start | bytes 3932160 | tf_op jit(solution)/shard_map/all_to_all | solution.py:829
  448.1 63.6 %collective-permute-start.40 = (bf16[15,96,512]{2,1,0:T(8,128)(2,1)}, bf16[15,96,512]{2,1,0:T(8,128)(2,1)}, u32[]{:S(2)}, u32[]{:S(2)}) collective-permute-start(bf16[15,96,512]{2,1,0:T(8,128)(2,1)} %pad_maximum_fusion.3), channel_id=1, source_target_pairs={{0,2},{1,3},{2,0},{3,1},{4,6},{5,7},{6,4},{7,5},{8,10},{9,11},{10,... | collective-permute-start | bytes 4423688 | tf_op jit(solution)/shard_map/ppermute | solution.py:62
  449.3 62.4 %collective-permute-start.39 = (bf16[15,96,512]{2,1,0:T(8,128)(2,1)}, bf16[15,96,512]{2,1,0:T(8,128)(2,1)}, u32[]{:S(2)}, u32[]{:S(2)}) collective-permute-start(bf16[15,96,512]{2,1,0:T(8,128)(2,1)} %pad_maximum_fusion.2), channel_id=1, source_target_pairs={{0,12},{1,13},{2,14},{3,15},{4,0},{5,1},{6,2},{7,3},{8,4},{9,5},{1... | collective-permute-start | bytes 4423688 | tf_op jit(solution)/shard_map/ppermute | solution.py:62
  449.8 61.9 %collective-permute-start.38 = (bf16[15,96,512]{2,1,0:T(8,128)(2,1)}, bf16[15,96,512]{2,1,0:T(8,128)(2,1)}, u32[]{:S(2)}, u32[]{:S(2)}) collective-permute-start(bf16[15,96,512]{2,1,0:T(8,128)(2,1)} %pad_maximum_fusion.1), channel_id=1, source_target_pairs={{0,4},{1,5},{2,6},{3,7},{4,8},{5,9},{6,10},{7,11},{8,12},{9,13},{1... | collective-permute-start | bytes 4423688 | tf_op jit(solution)/shard_map/ppermute | solution.py:62
  (73 other events, 1179.5 us)
Sparse Core Ops, SparseCore 0:
  12.6 55.9 all-gather.3
  70.4 128.7 all-gather.5
